TPU v7x, 32 devices: a whole 2x2x4 slice. The times are simulated.
32 devices in a mesh: prow: 4 (over x, core), pcol: 8 (over z, y).
Axes of the slice: x: 2, y: 2, z: 4, core: 2. Of those that a mesh axis runs over, the one named last changes fastest.
Arguments:
- basis: bfloat16 [512, 256], replicated, may hold values from -0.25 to 0.25
- potentials: float32 [8, 512], replicated, may hold values from -6 to 6
- orbitals: bfloat16 [64, 512], P('pcol'), may hold values from -6 to 6
- chan_orbital: int32 [128], replicated, may hold values from 0 to 63
- pair_list: int32 [6144, 3], P(('prow', 'pcol')), may hold values from 0 to 127, as said below
- slot_list: int32 [6144], P(('prow', 'pcol')), may hold values from 0 to 63
- coefs: float32 [6144, 2], P(('prow', 'pcol')), may hold values from -6 to 6
- exchange_ops: bfloat16 [6144, 128, 256], P(('prow', 'pcol')), may hold values from -1.1953125 to 1.1953125
Outputs:
- hamiltonian: bfloat16 [32, 4, 2, 8, 256, 256], P(None, 'prow', None, 'pcol')
Inputs may be any that keep to these rules, and one draw needn't show every extreme that they name: `pair_list`: columns 0 and 1 are channels a, b; column 2 is a multipole order below 8. (b // 8 - a // 8) modulo 128 // 8 is below 2. Terms of one device with the same slot s have the same two channels, and the block (a, b) belongs to owner s // 2 in prow-major order: a % 4 and b % 8 are that owner's prow and pcol indices.
All inputs are finite; a program needn't handle non-finite values.
Results may differ from a plain program's by a relative error of at most 0.0058.
Values may be sent and summed in bfloat16 or wider, within the bound.
A program may use at most 320 MiB of HBM per device.

v0:
```python
import jax
import jax.numpy as jnp
from jax import lax
from jax.sharding import PartitionSpec as P

CAP = 2
BAND = 2
RBLK = 32


def build_tiles(weights_group, exchange_group, basis):
    weights_group = lax.optimization_barrier(weights_group)
    scaled = (
        weights_group.astype(jnp.float32)[:, :, None] * basis.astype(jnp.float32)[None]
    ).astype(jnp.bfloat16)
    inner_rows = basis[: exchange_group.shape[1]]
    local_part = jnp.einsum("qa,gqb->gab", basis, scaled, preferred_element_type=jnp.float32)
    exchange_part = jnp.einsum(
        "qa,gqb->gab", inner_rows, exchange_group, preferred_element_type=jnp.float32
    )
    return (local_part + exchange_part).astype(jnp.bfloat16)


def sum_blocks(built_tiles, idents, block_count):
    select = (jnp.arange(block_count, dtype=jnp.int32)[:, None] == idents[None, :]).astype(
        jnp.bfloat16
    )
    spline_width = built_tiles.shape[1]
    summed = jnp.dot(
        select,
        built_tiles.reshape(built_tiles.shape[0], spline_width * spline_width),
        preferred_element_type=jnp.float32,
    )
    return summed.reshape(block_count, spline_width, spline_width)


def on_device(basis, potentials, orbitals, chan_orbital, pair_list, slot_list, coefs, exchange_ops):
    all_orbitals = lax.all_gather(orbitals, "pcol", axis=0, tiled=True)
    row_devs = lax.axis_size("prow")
    col_devs = lax.axis_size("pcol")
    slot_count = row_devs * col_devs * CAP
    chan_count = chan_orbital.shape[0]
    orb_count = all_orbitals.shape[0]
    point_count = basis.shape[0]
    spline_count = basis.shape[1]
    inner_count = exchange_ops.shape[1]
    term_count = exchange_ops.shape[0]
    col_groups = chan_count // col_devs
    block_count = RBLK * BAND
    first_chan = pair_list[:, 0]
    second_chan = pair_list[:, 1]
    multipole = pair_list[:, 2]
    channels = jnp.arange(chan_count, dtype=jnp.int32)
    orb_ids = jnp.arange(orb_count, dtype=jnp.int32)
    first_orb = jnp.sum(
        jnp.where(first_chan[:, None] == channels[None, :], chan_orbital[None, :], 0), axis=1
    )
    second_orb = jnp.sum(
        jnp.where(second_chan[:, None] == channels[None, :], chan_orbital[None, :], 0), axis=1
    )
    first_rows = jnp.dot(
        (first_orb[:, None] == orb_ids[None, :]).astype(jnp.bfloat16),
        all_orbitals,
        preferred_element_type=jnp.float32,
    )
    second_rows = jnp.dot(
        (second_orb[:, None] == orb_ids[None, :]).astype(jnp.bfloat16),
        all_orbitals,
        preferred_element_type=jnp.float32,
    )
    pick_pot = (
        multipole[:, None] == jnp.arange(potentials.shape[0], dtype=jnp.int32)[None, :]
    ).astype(jnp.float32)
    pot_rows = jnp.dot(pick_pot, potentials, precision=lax.Precision.HIGHEST)
    radial = coefs[:, 0:1] * pot_rows + coefs[:, 1:2] * (first_rows * second_rows)
    matches = slot_list[None, :] == jnp.arange(slot_count, dtype=jnp.int32)[:, None]
    slot_weight = jnp.dot(
        matches.astype(jnp.float32), radial, precision=lax.Precision.HIGHEST
    ).astype(jnp.bfloat16)
    exchange_rows = exchange_ops.reshape(term_count, inner_count * spline_count)
    slot_exchange = jnp.dot(
        matches.astype(jnp.bfloat16), exchange_rows, preferred_element_type=jnp.float32
    ).astype(jnp.bfloat16)
    slot_exchange = slot_exchange.reshape(slot_count, inner_count, spline_count)
    offset = jnp.mod(second_chan // col_devs - first_chan // col_devs, col_groups)
    block_index = first_chan // row_devs * BAND + offset
    slot_ids = jnp.max(jnp.where(matches, block_index[None, :], -1), axis=1)
    received, inner_received, idents = (
        lax.all_to_all(
            lax.all_to_all(
                slot_weight.reshape(row_devs, col_devs, CAP, point_count),
                "prow",
                split_axis=0,
                concat_axis=0,
                tiled=True,
            ),
            "pcol",
            split_axis=1,
            concat_axis=1,
            tiled=True,
        ),
        lax.all_to_all(
            lax.all_to_all(
                slot_exchange.reshape(row_devs, col_devs, CAP, inner_count, spline_count),
                "prow",
                split_axis=0,
                concat_axis=0,
                tiled=True,
            ),
            "pcol",
            split_axis=1,
            concat_axis=1,
            tiled=True,
        ),
        lax.all_to_all(
            lax.all_to_all(
                slot_ids.reshape(row_devs, col_devs, CAP),
                "prow",
                split_axis=0,
                concat_axis=0,
                tiled=True,
            ),
            "pcol",
            split_axis=1,
            concat_axis=1,
            tiled=True,
        ),
    )

    def accumulate(carried, inputs):
        weight_group, inner_group, group_ids = inputs
        return (
            carried
            + sum_blocks(build_tiles(weight_group, inner_group, basis), group_ids, block_count),
            None,
        )

    zeros_start = jnp.zeros((block_count, spline_count, spline_count), jnp.float32)
    blocks, unused = lax.scan(
        accumulate,
        zeros_start,
        (
            received.reshape(slot_count // 16, 16, point_count),
            inner_received.reshape(slot_count // 16, 16, inner_count, spline_count),
            idents.reshape(slot_count // 16, 16),
        ),
    )
    return blocks.astype(jnp.bfloat16).reshape(RBLK, 1, BAND, 1, spline_count, spline_count)


def solution(mesh):
    placed = (
        P(),
        P(),
        P("pcol", None),
        P(),
        P(("prow", "pcol"), None),
        P(("prow", "pcol")),
        P(("prow", "pcol"), None),
        P(("prow", "pcol"), None, None),
    )
    return jax.shard_map(
        on_device,
        mesh=mesh,
        in_specs=placed,
        out_specs=P(None, "prow", None, "pcol", None, None),
        check_vma=False,
    )
```

profile of v0, /device:TPU:0, one launch (start us, length us, event | category | flops | bytes accessed | tf_op | source)
XLA Modules:
  0.0 346.0 jit_solution(9799988007148520279)
XLA Ops:
  2.4 4.2 %all-to-all-start = ((s32[4,8,2]{1,2,0:T(2,128)}), s32[4,8,2]{1,2,0:T(2,128)S(1)}, u32[]{:S(2)}, u32[]{:S(2)}) async-start(s32[4,8,2]{1,2,0:T(2,128)} %copy.59), calls=%async_computation | async-start | bytes 8192 | tf_op jit(solution)/shard_map/all_to_all | solution.py:116
  8.3 31.5 %all_gather.3 = bf16[64,512]{1,0:T(8,128)(2,1)S(1)} all-gather(bf16[8,512]{1,0:T(8,128)(2,1)} %param.12), channel_id=1, replica_groups=mesh['prow'=4,'pcol'=8] {'pcol'}, dimensions={0}, use_global_device_ids=true | all-gather | bytes 73728 | tf_op jit(solution)/shard_map/all_gather | solution.py:38
  41.4 5.5 %all-to-all-start.1 = ((s32[4,8,2]{0,2,1:T(2,128)}), s32[4,8,2]{0,2,1:T(2,128)S(1)}, u32[]{:S(2)}, u32[]{:S(2)}) async-start(s32[4,8,2]{0,2,1:T(2,128)} %copy.60), calls=%async_computation.1 | async-start | bytes 16384 | tf_op jit(solution)/shard_map/all_to_all | solution.py:115
  48.5 13.9 %copy.72 = bf16[24,8,128,256]{3,1,2,0:T(8,128)(2,1)} copy(bf16[24,8,128,256]{3,2,1,0:T(8,128)(2,1)} %bitcast.75) | data formatting | bytes 25165824
  65.8 6.9 %convolution_convert_fusion = bf16[64,32768]{1,0:T(8,128)(2,1)S(1)} fusion(bf16[192,32768]{1,0:T(8,128)(2,1)} %bitcast.71, s32[192]{0:T(256)S(1)} %copy-done.3), kind=kOutput, calls=%fused_computation.21 | convolution fusion | flops 807415808 | bytes 16777984 | tf_op jit(solution)/shard_map/dot_general | solution.py:81
  75.8 4.8 %all-to-all-start.4 = ((bf16[4,8,2,128,256]{4,3,2,1,0:T(8,128)(2,1)}), bf16[4,8,2,128,256]{4,3,2,1,0:T(8,128)(2,1)}, u32[]{:S(2)}, u32[]{:S(2)}) async-start(bf16[4,8,2,128,256]{4,3,2,1,0:T(8,128)(2,1)} %bitcast.73), calls=%async_computation.4 | async-start | bytes 8388608 | tf_op jit(solution)/shard_map/all_to_all | solution.py:103
  81.3 47.6 %all-to-all-done.4 = bf16[4,8,2,128,256]{4,3,2,1,0:T(8,128)(2,1)} async-done(((bf16[4,8,2,128,256]{4,3,2,1,0:T(8,128)(2,1)}), bf16[4,8,2,128,256]{4,3,2,1,0:T(8,128)(2,1)}, u32[]{:S(2)}, u32[]{:S(2)}) %all-to-all-start.4) | async-done | bytes 4194336 | tf_op jit(solution)/shard_map/all_to_all | solution.py:103
  128.9 6.0 %all-to-all-start.3 = ((bf16[4,8,2,512]{3,2,0,1:T(2,128)(2,1)}), bf16[4,8,2,512]{3,2,0,1:T(2,128)(2,1)S(1)}, u32[]{:S(2)}, u32[]{:S(2)}) async-start(bf16[4,8,2,512]{3,2,0,1:T(2,128)(2,1)} %copy.61), calls=%async_computation.3 | async-start | bytes 131072 | tf_op jit(solution)/shard_map/all_to_all | solution.py:89
  134.9 4.7 %copy.63 = bf16[4,8,2,128,256]{4,3,2,0,1:T(8,128)(2,1)} copy(bf16[4,8,2,128,256]{4,3,2,1,0:T(8,128)(2,1)} %all-to-all-done.4) | data formatting | bytes 8388608 | tf_op jit(solution)/shard_map/all_to_all | solution.py:103
  141.8 4.7 %all-to-all-start.5 = ((bf16[4,8,2,128,256]{4,3,2,0,1:T(8,128)(2,1)}), bf16[4,8,2,128,256]{4,3,2,0,1:T(8,128)(2,1)}, u32[]{:S(2)}, u32[]{:S(2)}) async-start(bf16[4,8,2,128,256]{4,3,2,0,1:T(8,128)(2,1)} %copy.63), calls=%async_computation.5 | async-start | bytes 8388608 | tf_op jit(solution)/shard_map/all_to_all | solution.py:102
  146.7 91.5 %all-to-all-done.5 = bf16[4,8,2,128,256]{4,3,2,0,1:T(8,128)(2,1)} async-done(((bf16[4,8,2,128,256]{4,3,2,0,1:T(8,128)(2,1)}), bf16[4,8,2,128,256]{4,3,2,0,1:T(8,128)(2,1)}, u32[]{:S(2)}, u32[]{:S(2)}) %all-to-all-start.5) | async-done | bytes 4194336 | tf_op jit(solution)/shard_map/all_to_all | solution.py:102
  238.2 4.7 %copy.64 = bf16[4,8,2,128,256]{4,3,2,1,0:T(8,128)(2,1)} copy(bf16[4,8,2,128,256]{4,3,2,0,1:T(8,128)(2,1)} %all-to-all-done.5) | data formatting | bytes 8388608 | tf_op jit(solution)/shard_map/all_to_all | solution.py:102
  242.9 82.5 %while.11 = (s32[]{:T(128)}, f32[64,256,256]{2,0,1:T(8,128)}, s32[4,16]{1,0:T(4,128)S(1)}, bf16[4,16,512]{2,1,0:T(8,128)(2,1)S(1)}, bf16[512,256]{1,0:T(8,128)(2...) while((s32[]{:T(128)}, f32[64,256,256]{2,0,1:T(8,128)}, ...), condition=%wide.region_4.5_spmd.clone, body=%wide.region_3.4_spmd.clone.sunk | while | flops 1491084288 | bytes 53133616 | solution.py:139
  247.6 3.3 copy.84
  251.0 8.2 %select_add_fusion.2 = f32[64,256,256]{2,0,1:T(8,128)} fusion(f32[64,256,256]{2,0,1:T(8,128)} %get-tuple-element.160, pred[]{:T(512)S(6)} %compare.25, s32[16]{0:T(128)S(1)} %fusion.49, bf16[2,8,256,256]{3,1,2,0:T(8,128)(2,1)S(1)} %copy.84), kind=kOutput, calls=%fused_computation.clone.1 | convolution fusion | flops 142607360 | bytes 35651648 | tf_op jit(solution)/shard_map/while/body/eval_jaxpr/dot_general | solution.py:29
  263.9 3.3 copy.84
  267.3 14.0 %select_add_fusion.2 = f32[64,256,256]{2,0,1:T(8,128)} fusion(f32[64,256,256]{2,0,1:T(8,128)} %get-tuple-element.160, pred[]{:T(512)S(6)} %compare.25, s32[16]{0:T(128)S(1)} %fusion.49, bf16[2,8,256,256]{3,1,2,0:T(8,128)(2,1)S(1)} %copy.84), kind=kOutput, calls=%fused_computation.clone.1 | convolution fusion | flops 142607360 | bytes 35651648 | tf_op jit(solution)/shard_map/while/body/eval_jaxpr/dot_general | solution.py:29
  282.7 3.3 fusion.51
  286.0 3.3 copy.84
  289.3 14.0 %select_add_fusion.2 = f32[64,256,256]{2,0,1:T(8,128)} fusion(f32[64,256,256]{2,0,1:T(8,128)} %get-tuple-element.160, pred[]{:T(512)S(6)} %compare.25, s32[16]{0:T(128)S(1)} %fusion.49, bf16[2,8,256,256]{3,1,2,0:T(8,128)(2,1)S(1)} %copy.84), kind=kOutput, calls=%fused_computation.clone.1 | convolution fusion | flops 142607360 | bytes 35651648 | tf_op jit(solution)/shard_map/while/body/eval_jaxpr/dot_general | solution.py:29
  308.1 3.3 copy.84
  311.4 14.0 %select_add_fusion.2 = f32[64,256,256]{2,0,1:T(8,128)} fusion(f32[64,256,256]{2,0,1:T(8,128)} %get-tuple-element.160, pred[]{:T(512)S(6)} %compare.25, s32[16]{0:T(128)S(1)} %fusion.49, bf16[2,8,256,256]{3,1,2,0:T(8,128)(2,1)S(1)} %copy.84), kind=kOutput, calls=%fused_computation.clone.1 | convolution fusion | flops 142607360 | bytes 35651648 | tf_op jit(solution)/shard_map/while/body/eval_jaxpr/dot_general | solution.py:29
  325.4 9.1 %convert_element_type.36 = bf16[64,256,256]{2,0,1:T(8,128)(2,1)} convert(f32[64,256,256]{2,0,1:T(8,128)} %get-tuple-element.37) | non-fusion elementwise | flops 4194304 | bytes 25165824 | tf_op jit(solution)/shard_map/convert_element_type | solution.py:148
  334.4 11.6 %copy.68 = bf16[64,256,256]{2,1,0:T(8,128)(2,1)} copy(bf16[64,256,256]{2,0,1:T(8,128)(2,1)} %convert_element_type.36) | data formatting | bytes 16777216 | tf_op jit(solution)/shard_map/convert_element_type | solution.py:148
  (55 shorter events, 32.2 us)
Async XLA Ops:
  0.0 40.4 %copy-start = (f32[8,512]{1,0:T(8,128)S(1)}, f32[8,512]{1,0:T(8,128)}, u32[]{:S(2)}) copy-start(f32[8,512]{1,0:T(8,128)} %param.11) | copy-start | bytes 49156
  2.4 38.3 %all-to-all-start = ((s32[4,8,2]{1,2,0:T(2,128)}), s32[4,8,2]{1,2,0:T(2,128)S(1)}, u32[]{:S(2)}, u32[]{:S(2)}) async-start(s32[4,8,2]{1,2,0:T(2,128)} %copy.59), calls=%async_computation | async-start | bytes 8192 | tf_op jit(solution)/shard_map/all_to_all | solution.py:116
  41.4 21.0 %all-to-all-start.1 = ((s32[4,8,2]{0,2,1:T(2,128)}), s32[4,8,2]{0,2,1:T(2,128)S(1)}, u32[]{:S(2)}, u32[]{:S(2)}) async-start(s32[4,8,2]{0,2,1:T(2,128)} %copy.60), calls=%async_computation.1 | async-start | bytes 16384 | tf_op jit(solution)/shard_map/all_to_all | solution.py:115
  48.5 17.2 %copy-start.3 = (s32[192]{0:T(256)S(1)}, s32[192]{0:T(256)}, u32[]{:S(2)}) copy-start(s32[192]{0:T(256)} %param.15) | copy-start | bytes 2308
  62.5 13.3 %all-to-all-start.2 = ((bf16[4,8,2,512]{3,2,1,0:T(2,128)(2,1)}), bf16[4,8,2,512]{3,2,1,0:T(2,128)(2,1)S(1)}, u32[]{:S(2)}, u32[]{:S(2)}) async-start(bf16[4,8,2,512]{3,2,1,0:T(2,128)(2,1)} %reshape.116), calls=%async_computation.2 | async-start | bytes 131072 | tf_op jit(solution)/shard_map/all_to_all | solution.py:90
  75.8 53.1 %all-to-all-start.4 = ((bf16[4,8,2,128,256]{4,3,2,1,0:T(8,128)(2,1)}), bf16[4,8,2,128,256]{4,3,2,1,0:T(8,128)(2,1)}, u32[]{:S(2)}, u32[]{:S(2)}) async-start(bf16[4,8,2,128,256]{4,3,2,1,0:T(8,128)(2,1)} %bitcast.73), calls=%async_computation.4 | async-start | bytes 8388608 | tf_op jit(solution)/shard_map/all_to_all | solution.py:103
  128.9 12.9 %all-to-all-start.3 = ((bf16[4,8,2,512]{3,2,0,1:T(2,128)(2,1)}), bf16[4,8,2,512]{3,2,0,1:T(2,128)(2,1)S(1)}, u32[]{:S(2)}, u32[]{:S(2)}) async-start(bf16[4,8,2,512]{3,2,0,1:T(2,128)(2,1)} %copy.61), calls=%async_computation.3 | async-start | bytes 131072 | tf_op jit(solution)/shard_map/all_to_all | solution.py:89
  141.8 96.4 %all-to-all-start.5 = ((bf16[4,8,2,128,256]{4,3,2,0,1:T(8,128)(2,1)}), bf16[4,8,2,128,256]{4,3,2,0,1:T(8,128)(2,1)}, u32[]{:S(2)}, u32[]{:S(2)}) async-start(bf16[4,8,2,128,256]{4,3,2,0,1:T(8,128)(2,1)} %copy.63), calls=%async_computation.5 | async-start | bytes 8388608 | tf_op jit(solution)/shard_map/all_to_all | solution.py:102
  146.7 96.2 %copy-start.2 = (bf16[512,256]{1,0:T(8,128)(2,1)S(1)}, bf16[512,256]{1,0:T(8,128)(2,1)}, u32[]{:S(2)}) copy-start(bf16[512,256]{1,0:T(8,128)(2,1)} %param.10) | copy-start | bytes 786436
  334.4 11.6 %copy-start.1 = (f32[8,512]{1,0:T(8,128)S(1)}, f32[8,512]{1,0:T(8,128)}, u32[]{:S(2)}) copy-start(f32[8,512]{1,0:T(8,128)} %param.11) | copy-start | bytes 49156
where the time goes:
time: 347 us; the launch traced here: 346 us
  waiting for transfers between devices  141 us (41%)
  matrix products  77.1 us (22%)
  local copies, waits for them, and re-layouts  56.4 us (16%)
  blocking collectives  31.5 us (9%)
  starting transfers between devices  28.6 us (8%)
  other arithmetic  10.8 us (3%)
    all_to_all x1, waiting for transfers between devices, on_device(): lax.all_to_all(lax.all_to_all(slot_exchange.reshape(row_devs, col_devs, C...  91.5 us
    dot_general x4, matrix products, sum_blocks(): jnp.dot(select, built_tiles.reshape(built_tiles.shape[0], spline_width *...  50.1 us
    all_to_all x1, waiting for transfers between devices, on_device(): lax.all_to_all(slot_exchange.reshape(row_devs, col_devs, CAP, inner_count...  47.6 us
    all_gather x1, blocking collectives, on_device(): all_orbitals = lax.all_gather(orbitals, 'pcol', axis=0, tiled=True)  31.5 us
    unnamed x12, local copies, waits for them, and re-layouts  17.2 us
    while x4, local copies, waits for them, and re-layouts  13.4 us
    dot_general x4, matrix products, build_tiles(): jnp.einsum('qa,gqb->gab', inner_rows, exchange_group, preferred_element_t...  13.2 us
    convert_element_type x1, local copies, waits for them, and re-layouts, on_device(): blocks.astype(jnp.bfloat16)  11.6 us
  transfers between devices with their start and end apart: 6, of which 3 were waited for; matrix products, arithmetic and copies ran while one was open for 10% of the time, Pallas kernels for 0%

commit v1 on v0

v1 whole, which is shorter than its diff:
```python
import functools

import jax
import jax.numpy as jnp
from jax import lax
from jax.experimental import pallas as pl
from jax.experimental.pallas import tpu as pltpu
from jax.sharding import PartitionSpec as P

CAP = 2
BAND = 2
RBLK = 32
TERMS_STEP = 16
BLOCKS_STEP = 8
PACK = 16
VMEM_BYTES = 56 * 1024 * 1024
MESH = pl.DeviceIdType.MESH


def sum_slots_kernel(slot_smem, ops_ref, out_ref, acc):
    step = pl.program_id(0)
    slots = acc.shape[0]

    @pl.when(step == 0)
    def _():
        def clear(s, c):
            acc[s] = jnp.zeros(acc.shape[1:], jnp.float32)
            return c

        lax.fori_loop(0, slots, clear, 0)

    for i in range(TERMS_STEP):
        s = slot_smem[step * TERMS_STEP + i]
        acc[s] += ops_ref[i].astype(jnp.float32)

    @pl.when(step == pl.num_programs(0) - 1)
    def _():
        def convert(s, c):
            out_ref[s] = acc[s].astype(jnp.bfloat16)
            return c

        lax.fori_loop(0, slots, convert, 0)


def sum_slots(slot_list, exchange_ops, slot_count):
    terms, inner, width = exchange_ops.shape
    return pl.pallas_call(
        sum_slots_kernel,
        grid_spec=pltpu.PrefetchScalarGridSpec(
            num_scalar_prefetch=1,
            grid=(terms // TERMS_STEP,),
            in_specs=[pl.BlockSpec((TERMS_STEP, inner, width), lambda i, s: (i, 0, 0))],
            out_specs=pl.BlockSpec((slot_count, inner, width), lambda i, s: (0, 0, 0)),
            scratch_shapes=[pltpu.VMEM((slot_count, inner, width), jnp.float32)],
        ),
        out_shape=jax.ShapeDtypeStruct((slot_count, inner, width), jnp.bfloat16),
        compiler_params=pltpu.CompilerParams(
            dimension_semantics=("arbitrary",), vmem_limit_bytes=VMEM_BYTES
        ),
        name="sum_slots",
    )(slot_list, exchange_ops)


def exchange_kernel(
    nrow,
    ncol,
    col_groups,
    orb_per,
    exch_ref,
    orb_ref,
    pot_ref,
    chan_ref,
    rows_ref,
    pair_ref,
    coef_ref,
    recv_ref,
    wrecv_ref,
    all_orb,
    wsend,
    orb_ssem,
    orb_rsem,
    w_ssem,
    w_rsem,
    e_ssem,
    e_rsem,
    own_sem,
):
    p = lax.axis_index("prow")
    q = lax.axis_index("pcol")
    ndev = nrow * ncol
    me = p * ncol + q
    f32 = jnp.float32

    def peer(t):
        dq = lax.rem(t * (ncol // 2 + 1), ncol)
        dp = lax.rem(lax.div(t, ncol) + t, nrow)
        return lax.rem(p + dp, nrow), lax.rem(q + dq, ncol)

    barrier = pltpu.get_barrier_semaphore()

    def greet(t, c):
        pp, qq = peer(t)
        pl.semaphore_signal(barrier, inc=1, device_id=(pp, qq), device_id_type=MESH)
        return c

    lax.fori_loop(1, ndev, greet, 0)
    pl.semaphore_wait(barrier, ndev - 1)

    def orb_copy(t):
        return pltpu.make_async_remote_copy(
            src_ref=orb_ref,
            dst_ref=all_orb.at[q],
            send_sem=orb_ssem.at[t],
            recv_sem=orb_rsem.at[t],
            device_id=(p, lax.rem(q + t, ncol)),
            device_id_type=MESH,
        )

    def exch_copy(t):
        pp, qq = peer(t)
        return pltpu.make_async_remote_copy(
            src_ref=exch_ref.at[pp * ncol + qq],
            dst_ref=recv_ref.at[me],
            send_sem=e_ssem.at[t],
            recv_sem=e_rsem.at[t],
            device_id=(pp, qq),
            device_id_type=MESH,
        )

    def weight_copy(t):
        pp, qq = peer(t)
        return pltpu.make_async_remote_copy(
            src_ref=wsend.at[pp * ncol + qq],
            dst_ref=wrecv_ref.at[me],
            send_sem=w_ssem.at[t],
            recv_sem=w_rsem.at[t],
            device_id=(pp, qq),
            device_id_type=MESH,
        )

    def each(count, action):
        def body(t, c):
            action(t)
            return c

        lax.fori_loop(1, count, body, 0)

    each(ncol, lambda t: orb_copy(t).start())
    each(ndev, lambda t: exch_copy(t).start())
    own = pltpu.make_async_copy(exch_ref.at[me], recv_ref.at[me], own_sem.at[0])
    own.start()
    each(ncol, lambda t: orb_copy(t).wait())
    all_orb[q] = orb_ref[...]

    terms = pair_ref.shape[0]
    points = orb_ref.shape[1]
    chans = chan_ref.shape[1]
    orbs = all_orb[...].reshape(ncol * all_orb.shape[1], points).astype(jnp.bfloat16)
    chan_iota = lax.broadcasted_iota(jnp.int32, (terms, chans), 1)
    orb_iota = lax.broadcasted_iota(jnp.int32, (terms, orbs.shape[0]), 1)

    def pick(column):
        chan = pair_ref[:, column : column + 1]
        orb = jnp.sum(jnp.where(chan_iota == chan, chan_ref[...], 0), axis=1, keepdims=True)
        place = orb // orb_per * all_orb.shape[1] + orb % orb_per
        hot = jnp.where(orb_iota == place, 1.0, 0.0).astype(jnp.bfloat16)
        return jnp.dot(hot, orbs, preferred_element_type=f32)

    pot = jnp.zeros((terms, points), f32)
    multipole = pair_ref[:, 2:3]
    for l in range(pot_ref.shape[0]):
        pot = jnp.where(multipole == l, pot_ref[l : l + 1, :], pot)
    radial = coef_ref[:, 0:1] * pot + coef_ref[:, 1:2] * (pick(0) * pick(1))

    pieces = points // 128
    lines = ndev * PACK
    line = lax.broadcasted_iota(jnp.int32, (lines, terms), 0)
    inside = line % PACK
    line_slot = line // PACK * CAP + inside % (CAP * pieces) // pieces
    match = line_slot == rows_ref[0:1, :]
    is_weight = inside < CAP * pieces
    total = jnp.zeros((lines, 128), f32)
    for j in range(pieces):
        hot = jnp.where(match & is_weight & (inside % pieces == j), 1.0, 0.0).astype(f32)
        total += jnp.dot(
            hot,
            radial[:, j * 128 : (j + 1) * 128],
            precision=lax.Precision.HIGHEST,
            preferred_element_type=f32,
        )
    first = rows_ref[1:2, :]
    second = rows_ref[2:3, :]
    offset = (second // ncol - first // ncol + col_groups) % col_groups
    block = (first // nrow * BAND + offset).astype(f32)
    ids = jnp.max(jnp.where(match, block, -1.0), axis=1, keepdims=True)
    line_col = lax.broadcasted_iota(jnp.int32, (lines, 128), 0) % PACK
    total = jnp.where(line_col < CAP * pieces, total, ids)
    wsend[...] = total.astype(jnp.bfloat16).reshape(ndev, PACK, 128)

    each(ndev, lambda t: weight_copy(t).start())
    own_w = pltpu.make_async_copy(wsend.at[me], wrecv_ref.at[me], own_sem.at[1])
    own_w.start()
    each(ndev, lambda t: exch_copy(t).wait())
    each(ndev, lambda t: weight_copy(t).wait())
    own.wait()
    own_w.wait()


def exchange(nrow, ncol, col_groups, slot_sums, orb, potentials, chan, rows, pairs, coefs, orb_per):
    ndev = nrow * ncol
    inner, width = slot_sums.shape[1:]
    any_spec = pl.BlockSpec(memory_space=pl.ANY)
    vmem = pl.BlockSpec(memory_space=pltpu.VMEM)
    dma = pltpu.SemaphoreType.DMA
    return pl.pallas_call(
        functools.partial(exchange_kernel, nrow, ncol, col_groups, orb_per),
        out_shape=(
            jax.ShapeDtypeStruct((ndev, CAP, inner, width), jnp.bfloat16),
            jax.ShapeDtypeStruct((ndev, PACK, 128), jnp.bfloat16),
        ),
        in_specs=[any_spec] + [vmem] * 6,
        out_specs=(any_spec, any_spec),
        scratch_shapes=[
            pltpu.VMEM((ncol,) + orb.shape, jnp.float32),
            pltpu.VMEM((ndev, PACK, 128), jnp.bfloat16),
            dma((ncol,)),
            dma((ncol,)),
            dma((ndev,)),
            dma((ndev,)),
            dma((ndev,)),
            dma((ndev,)),
            dma((2,)),
        ],
        compiler_params=pltpu.CompilerParams(
            collective_id=0, has_side_effects=True, vmem_limit_bytes=VMEM_BYTES
        ),
        name="exchange",
    )(slot_sums.reshape(ndev, CAP, inner, width), orb, potentials, chan, rows, pairs, coefs)


def blocks_kernel(
    ids_smem, recv_ref, wrecv_ref, basis_ref, basis_t_ref, out_ref, weights, heads, nexts, sums
):
    step = pl.program_id(0)
    slots = recv_ref.shape[0]
    blocks = heads.shape[0]
    inner, width = recv_ref.shape[1:]
    ndev = wrecv_ref.shape[0]
    pieces = basis_ref.shape[0] // 128
    half = CAP * pieces
    f32 = jnp.float32

    @pl.when(step == 0)
    def _():
        def clear(t, c):
            heads[t] = -1
            return c

        lax.fori_loop(0, blocks, clear, 0)

        def link(s, c):
            t = ids_smem[s]

            @pl.when(t >= 0)
            def _():
                nexts[s] = heads[t]
                heads[t] = s

            return c

        lax.fori_loop(0, slots, link, 0)
        packed = wrecv_ref[...].astype(f32)
        values = packed[:, :half, :].reshape(ndev * half, 128).astype(jnp.bfloat16)
        ids = packed[:, half:, :].reshape(ndev * half, 128)
        lane = lax.broadcasted_iota(jnp.int32, ids.shape, 1).astype(f32)
        piece = lax.broadcasted_iota(jnp.int32, ids.shape, 0) % pieces
        for j in range(pieces):
            hot = jnp.where((ids == lane) & (piece == j), 1.0, 0.0).astype(jnp.bfloat16)
            weights[:, j * 128 : (j + 1) * 128] = lax.dot_general(
                hot, values, (((0,), (0,)), ((), ())), preferred_element_type=f32
            )[:blocks]

    for i in range(BLOCKS_STEP):
        t = step * BLOCKS_STEP + i
        head = heads[t]

        @pl.when(head < 0)
        def _():
            out_ref[i] = jnp.zeros(out_ref.shape[1:], out_ref.dtype)

        @pl.when(head >= 0)
        def _():
            sums[...] = recv_ref[head].astype(f32)

            def more(s):
                sums[...] += recv_ref[s].astype(f32)
                return nexts[s]

            lax.while_loop(lambda s: s >= 0, more, nexts[head])
            scaled = (basis_t_ref[...].astype(f32) * weights[pl.ds(t, 1), :]).astype(jnp.bfloat16)
            local = jnp.dot(scaled, basis_ref[...], preferred_element_type=f32)
            swapped = jnp.dot(
                basis_t_ref[:, :inner], sums[...].astype(jnp.bfloat16), preferred_element_type=f32
            )
            out_ref[i] = (local + swapped).astype(out_ref.dtype)


def make_blocks(ids, received, packed, basis, basis_t):
    slots, inner, width = received.shape
    blocks = RBLK * BAND
    points = basis.shape[0]
    whole = lambda a: pl.BlockSpec(a.shape, lambda i, s: (0,) * a.ndim)
    return pl.pallas_call(
        blocks_kernel,
        grid_spec=pltpu.PrefetchScalarGridSpec(
            num_scalar_prefetch=1,
            grid=(blocks // BLOCKS_STEP,),
            in_specs=[whole(received), whole(packed), whole(basis), whole(basis_t)],
            out_specs=pl.BlockSpec((BLOCKS_STEP, width, width), lambda i, s: (i, 0, 0)),
            scratch_shapes=[
                pltpu.VMEM((blocks, points), jnp.float32),
                pltpu.SMEM((blocks,), jnp.int32),
                pltpu.SMEM((slots,), jnp.int32),
                pltpu.VMEM((inner, width), jnp.float32),
            ],
        ),
        out_shape=jax.ShapeDtypeStruct((blocks, width, width), jnp.bfloat16),
        compiler_params=pltpu.CompilerParams(
            dimension_semantics=("arbitrary",), vmem_limit_bytes=VMEM_BYTES
        ),
        name="make_blocks",
    )(ids, received, packed, basis, basis_t)


def on_device(basis, potentials, orbitals, chan_orbital, pair_list, slot_list, coefs, exchange_ops):
    nrow = lax.axis_size("prow")
    ncol = lax.axis_size("pcol")
    slot_count = nrow * ncol * CAP
    inner, width = exchange_ops.shape[1:]
    orb_per = orbitals.shape[0]
    padding = -orb_per % 8
    orb = jnp.pad(orbitals.astype(jnp.float32), ((0, padding), (0, 0)))
    rows = jnp.concatenate([slot_list[None, :], pair_list.T], axis=0)
    slot_sums = sum_slots(slot_list, exchange_ops, slot_count)
    received, packed = exchange(
        nrow,
        ncol,
        chan_orbital.shape[0] // ncol,
        slot_sums,
        orb,
        potentials,
        chan_orbital[None, :],
        rows,
        pair_list,
        coefs,
        orb_per,
    )
    pieces = basis.shape[0] // 128
    ids = packed[:, CAP * pieces :: pieces, 0].astype(jnp.int32).reshape(slot_count)
    blocks = make_blocks(ids, received.reshape(slot_count, inner, width), packed, basis, basis.T)
    return blocks.reshape(RBLK, 1, BAND, 1, width, width)


def solution(mesh):
    placed = (
        P(),
        P(),
        P("pcol", None),
        P(),
        P(("prow", "pcol"), None),
        P(("prow", "pcol")),
        P(("prow", "pcol"), None),
        P(("prow", "pcol"), None, None),
    )
    return jax.shard_map(
        on_device,
        mesh=mesh,
        in_specs=placed,
        out_specs=P(None, "prow", None, "pcol", None, None),
        check_vma=False,
    )
```

time: 347 us -> 147 us (0.42)
  waiting for transfers between devices: 141 us -> 0 us
  Pallas kernels: 0 us -> 137 us
  matrix products: 77.1 us -> 0 us
  local copies, waits for them, and re-layouts: 56.4 us -> 6.14 us
  blocking collectives: 31.5 us -> 0 us
  starting transfers between devices: 28.6 us -> 0 us
  other arithmetic: 10.8 us -> 3.2 us
    all_to_all x6 -> x0, waiting for transfers between devices: 141 us -> none  [the longest x1 91.5 us: on_device(): lax.all_to_all(lax.all_to_all(slot_exchange.reshape(row_devs, col_devs, C...]
    pallas_call x0 -> x3, Pallas kernels: none -> 137 us  [the longest x1 108 us: exchange(): pl.pallas_call(functools.partial(exchange_kernel, nrow, ncol, col_groups,...]
    dot_general x17 -> x0, matrix products: 77.1 us -> none  [the longest x4 50.1 us: sum_blocks(): jnp.dot(select, built_tiles.reshape(built_tiles.shape[0], spline_width *...]
    all_gather x1 -> x0, blocking collectives: 31.5 us -> none  [on_device(): all_orbitals = lax.all_gather(orbitals, 'pcol', axis=0, tiled=True)]
    all_to_all x6 -> x0, starting transfers between devices: 28.6 us -> none  [the longest x1 6 us: on_device(): lax.all_to_all(lax.all_to_all(slot_weight.reshape(row_devs, col_devs, CAP...]
    while x4 -> x0, local copies, waits for them, and re-layouts: 13.4 us -> none
    unnamed x12 -> x3, local copies, waits for them, and re-layouts: 17.2 us -> 4.66 us
    convert_element_type x5 -> x1, local copies, waits for them, and re-layouts: 12.1 us -> 0.62 us  [on_device(): packed[:, CAP * pieces::pieces, 0].astype(jnp.int32).reshape(slot_count)]
  transfers between devices with their start and end apart: 6 -> 0, of which waited for: 3 -> 0; matrix products, arithmetic and copies ran while one was open for 10% -> 0% of each run, Pallas kernels for 0% -> 0%
where the time goes in v1:
time: 147 us
  Pallas kernels  137 us (93%)
  local copies, waits for them, and re-layouts  6.14 us (4%)
  other arithmetic  3.2 us (2%)
    pallas_call x1, Pallas kernels, exchange(): pl.pallas_call(functools.partial(exchange_kernel, nrow, ncol, col_groups,...  108 us
    pallas_call x1, Pallas kernels, make_blocks(): pl.pallas_call(blocks_kernel, grid_spec=pltpu.PrefetchScalarGridSpec(num_...  16.3 us
    pallas_call x1, Pallas kernels, sum_slots(): pl.pallas_call(sum_slots_kernel, grid_spec=pltpu.PrefetchScalarGridSpec(n...  13.3 us
    unnamed x3, local copies, waits for them, and re-layouts  4.66 us

profile of v1, /device:TPU:0, one launch (start us, length us, event | category | flops | bytes accessed | tf_op | source)
XLA Modules:
  0.0 146.5 jit_solution(10843697293854412412)
XLA Ops:
  0.0 1.3 pad_add_fusion.rows_ref
  1.3 1.3 convert_element_type.10.orb_ref
  2.6 1.4 copy.14.coef_ref
  4.0 1.4 copy.13.pair_ref
  5.5 1.8 %copy.15 = bf16[512,256]{0,1:T(8,128)(2,1)} copy(bf16[512,256]{1,0:T(8,128)(2,1)} %basis_ref.1) | data formatting | bytes 524288 | tf_op args[0]
  7.3 13.3 %sum_slots.1 = bf16[64,128,256]{2,1,0:T(8,128)(2,1)} custom-call(s32[192]{0:T(256)} %slot_smem.1, bf16[192,128,256]{2,1,0:T(8,128)(2,1)} %ops_ref.1), custom_call_target="tpu_custom_call" | custom-call | tf_op jit(solution)/shard_map/sum_slots/pallas_call | solution.py:47
  20.5 107.6 %exchange.1 = (bf16[32,2,128,256]{3,2,1,0:T(8,128)(2,1)}, bf16[32,16,128]{2,1,0:T(8,128)(2,1)}) custom-call(bf16[32,2,128,256]{3,2,1,0:T(8,128)(2,1)} %bitcast.9, f32[8,512]{1,0:T(8,128)} %convert_element_type.10.orb_ref, f32[8,512]{1,0:T(8,128)} %pot_ref.1, s32[1,128]{1,0:T(1,128)} %bitcast.14, s32[4,192]{1,0:T(4,128)} %pad_add_fusion.rows_ref, ...), custom_call_target="tpu_custom_call" | custom-call | tf_op jit(solution)/shard_map/exchange/pallas_call | solution.py:215
  128.2 0.9 slice.3
  129.0 0.6 convert_reduce_fusion
  129.6 0.6 reshape.16.ids_smem
  130.3 16.3 %make_blocks.1 = bf16[64,256,256]{2,1,0:T(8,128)(2,1)} custom-call(s32[64]{0:T(128)} %reshape.16.ids_smem, bf16[64,128,256]{2,1,0:T(8,128)(2,1)} %bitcast.10, bf16[32,16,128]{2,1,0:T(8,128)(2,1)} %get-tuple-element.7.wrecv_ref, bf16[512,256]{1,0:T(8,128)(2,1)} %basis_ref.1, bf16[256,512]{1,0:T(8,128)(2,1)} %bitcast.11), custom_call_target="tpu_custom_call" | custom-call | tf_op jit(solution)/shard_map/make_blocks/pallas_call | solution.py:313

commit v2 on v0

v2 whole, which is shorter than its diff:
```python
import functools

import jax
import jax.numpy as jnp
from jax import lax
from jax.experimental import pallas as pl
from jax.experimental.pallas import tpu as pltpu
from jax.sharding import PartitionSpec as P

CAP = 2
BAND = 2
RBLK = 32
BLOCKS_STEP = 8
FIRST_ROWS = 32
SPAN = 16
VMEM_BYTES = 56 * 1024 * 1024
MESH = pl.DeviceIdType.MESH
EXACT = lax.Precision.HIGHEST
FAR = 1.0e6


def product(left, right, left_dim, right_dim, precision=None):
    return lax.dot_general(
        left,
        right,
        (((left_dim,), (right_dim,)), ((), ())),
        precision=precision,
        preferred_element_type=jnp.float32,
    )


def iota(shape, dim):
    return lax.broadcasted_iota(jnp.int32, shape, dim)


def turned(row):
    n = row.shape[1]
    same = iota((n, n), 0) == iota((n, n), 1)
    return jnp.sum(jnp.where(same, row, jnp.zeros_like(row)), axis=1, keepdims=True)


def slot_order(slot, slots, table):
    n = slot.shape[1]
    col = turned(slot)
    under, over = iota((n, n), 0), iota((n, n), 1)
    same = col == slot
    rank = jnp.sum(jnp.where((col < slot) | (same & (under < over)), 1, 0), axis=0, keepdims=True)
    place = turned(rank) == over
    before = jnp.sum(jnp.where(same & (over < under), 1, 0), axis=1, keepdims=True)
    order = jnp.sum(jnp.where(place, under, 0), axis=0, keepdims=True)
    keeps = jnp.sum(jnp.where(place, before, 0), axis=0, keepdims=True)
    upto = jnp.where(col <= iota((n, slots), 1), 1, 0)
    last = jnp.sum(upto, axis=0, keepdims=True) - 1
    table[...] = jnp.zeros_like(table)
    table[0:1, :n] = order
    table[1:2, :n] = keeps
    table[2:3, :slots] = last


def exchange_kernel(
    nrow,
    ncol,
    ops_ref,
    orb_ref,
    pot_ref,
    chan_ref,
    slot_ref,
    pair_ref,
    coef_ref,
    basis_ref,
    recv_ref,
    local_ref,
    lists_ref,
    terms_a,
    terms_b,
    running,
    send_a,
    send_b,
    orb_wide,
    orb_send,
    all_orb,
    msg_send,
    msg_recv,
    pot_pad,
    basis_t,
    weights,
    local_blocks,
    table,
    order_smem,
    orb_ssem,
    orb_rsem,
    m_ssem,
    m_rsem,
    e_ssem,
    e_rsem,
    own_sem,
):
    p = lax.axis_index("prow")
    q = lax.axis_index("pcol")
    ndev = nrow * ncol
    me = p * ncol + q
    f32 = jnp.float32
    bf16 = jnp.bfloat16
    slots = ndev * CAP
    blocks = RBLK * BAND
    terms = slot_ref.shape[1]
    chans = chan_ref.shape[1]
    groups = chans // ncol
    points = pot_ref.shape[1]
    orb_per = orb_ref.shape[0]
    orb_rows = orb_wide.shape[0]
    top = terms - 1
    chunks = ((terms_a, send_a, 0), (terms_b, send_b, FIRST_ROWS))

    def peer(t):
        dq = lax.rem(t * (ncol // 2 + 1), ncol)
        dp = lax.rem(lax.div(t, ncol) + t, nrow)
        return lax.rem(p + dp, nrow), lax.rem(q + dq, ncol)

    def each(count, action):
        def body(t, c):
            action(t)
            return c

        lax.fori_loop(1, count, body, 0)

    def load(c):
        buffer, _, start = chunks[c]
        return pltpu.make_async_copy(
            ops_ref.at[:, pl.ds(start, buffer.shape[1]), :], buffer, own_sem.at[c]
        )

    def remote(source, target, sems, t, device):
        return pltpu.make_async_remote_copy(
            src_ref=source,
            dst_ref=target,
            send_sem=sems[0].at[t],
            recv_sem=sems[1].at[t],
            device_id=device,
            device_id_type=MESH,
        )

    def orb_copy(t):
        return remote(
            orb_send, all_orb.at[q], (orb_ssem, orb_rsem), t, (p, lax.rem(q + t, ncol))
        )

    def msg_copy(t):
        pp, qq = peer(t)
        return remote(
            msg_send.at[pp * ncol + qq], msg_recv.at[me], (m_ssem, m_rsem), t, (pp, qq)
        )

    def landing(c):
        _, send, start = chunks[c]
        return recv_ref.at[me, :, pl.ds(start, send.shape[2]), :]

    def exch_copy(c, t):
        pp, qq = peer(t)
        return remote(
            chunks[c][1].at[pp * ncol + qq],
            landing(c),
            (e_ssem.at[c], e_rsem.at[c]),
            t,
            (pp, qq),
        )

    def own_copy(c):
        return pltpu.make_async_copy(chunks[c][1].at[me], landing(c), own_sem.at[2 + c])

    load(0).start()
    load(1).start()
    barrier = pltpu.get_barrier_semaphore()
    each(
        ndev,
        lambda t: pl.semaphore_signal(barrier, inc=1, device_id=peer(t), device_id_type=MESH),
    )

    orb_wide[...] = jnp.zeros_like(orb_wide)
    orb_wide[:orb_per, :] = orb_ref[...].astype(f32)
    orb_send[...] = jnp.concatenate(
        [orb_wide[:, : points // 2], orb_wide[:, points // 2 :]], axis=0
    ).astype(bf16)

    slot = slot_ref[...]
    first, second, multipole = pair_ref[0:1, :], pair_ref[1:2, :], pair_ref[2:3, :]
    offset = (second // ncol - first // ncol + groups) % groups
    block = (first // nrow * BAND + offset).astype(f32)
    kind = iota((128, terms), 0)
    lane = iota((ndev, 128), 1)
    message = jnp.zeros((ndev, 128), f32)
    for c in range(CAP):
        base = SPAN * c
        parts = jnp.where(kind == multipole + base, coef_ref[0:1, :], 0.0)
        parts = jnp.where(kind == base + 8, coef_ref[1:2, :], parts)
        match = slot == iota((ndev, terms), 0) * CAP + c
        message += product(jnp.where(match, 1.0, 0.0), parts, 1, 1, EXACT)
        number = jnp.max(jnp.where(match, block, -1.0), axis=1, keepdims=True)
        message = jnp.where(lane == base + 9, number, message)
    msg_send[...] = message.reshape(ndev, 1, 128)

    slot_order(slot, slots, table)
    order_copy = pltpu.make_async_copy(table, order_smem, own_sem.at[4])
    order_copy.start()
    pl.semaphore_wait(barrier, ndev - 1)
    each(ncol, lambda t: orb_copy(t).start())
    each(ndev, lambda t: msg_copy(t).start())
    order_copy.wait()

    for c, (buffer, send, _) in enumerate(chunks):
        height, width = buffer.shape[1:]
        load(c).wait()

        def add(i, total):
            kept = jnp.where(order_smem[1, i] > 0, total, jnp.zeros_like(total))
            total = kept + buffer[jnp.clip(order_smem[0, i], 0, top)].astype(f32)
            running[i, :height, :] = total.astype(bf16)
            return total

        lax.fori_loop(0, terms, add, jnp.zeros((height, width), f32), unroll=4)

        def place(o, carried):
            for k in range(CAP):
                end = jnp.clip(order_smem[2, o * CAP + k], 0, top)
                send[o, k] = running[end, :height, :]
            return carried

        lax.fori_loop(0, ndev, place, 0)
        each(ndev, lambda t: exch_copy(c, t).start())
        own_copy(c).start()

    each(ncol, lambda t: orb_copy(t).wait())
    all_orb[q] = orb_send[...]
    each(ndev, lambda t: msg_copy(t).wait())
    msg_recv[me] = msg_send[me]

    wide = all_orb[...].astype(f32)
    orbs = jnp.concatenate(
        [
            wide[:, :orb_rows, :].reshape(ncol * orb_rows, points // 2),
            wide[:, orb_rows:, :].reshape(ncol * orb_rows, points // 2),
        ],
        axis=1,
    ).astype(bf16)
    chan_row = chan_ref[...]
    chan_place = chan_row // orb_per * orb_rows + chan_row % orb_per
    owns = jnp.where(iota((ncol * orb_rows, chans), 0) == chan_place, 1.0, 0.0).astype(bf16)
    number = iota((128, chans), 0)
    first_chan = number // BAND * nrow + p
    second_chan = (first_chan // ncol + number % BAND) % groups * ncol + q

    def orbital_of(chan):
        hot = jnp.where(iota((128, chans), 1) == chan, 1.0, 0.0).astype(bf16)
        return product(product(hot, owns, 1, 1).astype(bf16), orbs, 1, 0)

    received = msg_recv[...].reshape(ndev, 128)
    numbers = []
    sums = jnp.zeros((128, 128), f32)
    for c in range(CAP):
        base = SPAN * c
        ids = jnp.sum(jnp.where(lane == base + 9, received, 0.0), axis=1, keepdims=True)
        numbers.append(ids)
        hot = jnp.where(lane.astype(f32) == ids, 1.0, 0.0)
        inside = (lane >= base) & (lane < base + 9)
        sums += product(hot, jnp.where(inside, received, 0.0), 0, 0, EXACT)
    pot_pad[...] = jnp.zeros_like(pot_pad)
    for c in range(CAP):
        pot_pad[SPAN * c : SPAN * c + 8, :] = pot_ref[...]
    lanes = iota((128, 128), 1)
    factor = jnp.sum(jnp.where(lanes % SPAN == 8, sums, 0.0), axis=1, keepdims=True)
    weights[...] = product(sums, pot_pad[...], 1, 0, EXACT) + factor * (
        orbital_of(first_chan) * orbital_of(second_chan)
    )

    size = lists_ref.shape[1]
    source = iota((ndev, size), 0)
    spot = iota((ndev, size), 1)
    row = jnp.full((1, size), -1.0, f32)
    for c in range(CAP):
        row += jnp.sum(
            jnp.where(spot == source * CAP + c, numbers[c] + 1.0, 0.0), axis=0, keepdims=True
        )
    col = turned(row)
    under = iota((size, size), 0).astype(f32)
    over = iota((size, size), 1).astype(f32)
    heads = jnp.min(jnp.where(col == over, under, FAR), axis=0, keepdims=True)
    nexts = jnp.min(jnp.where((col == row) & (under > over), under, FAR), axis=0, keepdims=True)
    lists_ref[...] = jnp.zeros_like(lists_ref)
    lists_ref[0:1, :] = jnp.where(heads < FAR, heads, -1.0).astype(jnp.int32)
    lists_ref[1:2, :] = jnp.where(nexts < FAR, nexts, -1.0).astype(jnp.int32)

    basis_t[...] = basis_ref[...].astype(f32).T

    def form(t, carried):
        scaled = (basis_t[...] * weights[pl.ds(t, 1), :]).astype(bf16)
        local_blocks[t] = jnp.dot(
            scaled, basis_ref[...], preferred_element_type=f32
        ).astype(bf16)
        return carried

    lax.fori_loop(0, blocks, form, 0)
    out_copy = pltpu.make_async_copy(local_blocks, local_ref, own_sem.at[5])
    out_copy.start()
    for c in range(len(chunks)):
        each(ndev, lambda t: exch_copy(c, t).wait())
        own_copy(c).wait()
    out_copy.wait()


def exchange(nrow, ncol, exchange_ops, orbitals, potentials, chan, slot, pairs, coefs, basis):
    ndev = nrow * ncol
    terms, inner, width = exchange_ops.shape
    points = basis.shape[0]
    blocks = RBLK * BAND
    orb_rows = -(-orbitals.shape[0] // 8) * 8
    size = -(-max(ndev * CAP, 128) // 128) * 128
    span = -(-max(ndev * CAP, terms) // 128) * 128
    rest = inner - FIRST_ROWS
    any_spec = pl.BlockSpec(memory_space=pl.ANY)
    vmem = pl.BlockSpec(memory_space=pltpu.VMEM)
    dma = pltpu.SemaphoreType.DMA
    f32, bf16 = jnp.float32, jnp.bfloat16
    return pl.pallas_call(
        functools.partial(exchange_kernel, nrow, ncol),
        out_shape=(
            jax.ShapeDtypeStruct((ndev, CAP, inner, width), bf16),
            jax.ShapeDtypeStruct((blocks, width, width), bf16),
            jax.ShapeDtypeStruct((8, size), jnp.int32),
        ),
        in_specs=[any_spec] + [vmem] * 7,
        out_specs=(any_spec, any_spec, vmem),
        scratch_shapes=[
            pltpu.VMEM((terms, FIRST_ROWS, width), bf16),
            pltpu.VMEM((terms, rest, width), bf16),
            pltpu.VMEM((terms, max(rest, FIRST_ROWS), width), bf16),
            pltpu.VMEM((ndev, CAP, FIRST_ROWS, width), bf16),
            pltpu.VMEM((ndev, CAP, rest, width), bf16),
            pltpu.VMEM((orb_rows, points), f32),
            pltpu.VMEM((2 * orb_rows, points // 2), bf16),
            pltpu.VMEM((ncol, 2 * orb_rows, points // 2), bf16),
            pltpu.VMEM((ndev, 1, 128), f32),
            pltpu.VMEM((ndev, 1, 128), f32),
            pltpu.VMEM((128, points), f32),
            pltpu.VMEM((width, points), f32),
            pltpu.VMEM((128, points), f32),
            pltpu.VMEM((blocks, width, width), bf16),
            pltpu.VMEM((8, span), jnp.int32),
            pltpu.SMEM((8, span), jnp.int32),
            dma((ncol,)),
            dma((ncol,)),
            dma((ndev,)),
            dma((ndev,)),
            dma((2, ndev)),
            dma((2, ndev)),
            dma((6,)),
        ],
        compiler_params=pltpu.CompilerParams(
            collective_id=0, has_side_effects=True, vmem_limit_bytes=VMEM_BYTES
        ),
        name="exchange",
    )(exchange_ops, orbitals, potentials, chan, slot, pairs, coefs, basis)


def blocks_kernel(lists_smem, recv_ref, inner_ref, local_ref, out_ref, inner_t, sums, joined):
    step = pl.program_id(0)
    f32 = jnp.float32

    @pl.when(step == 0)
    def _():
        inner_t[...] = inner_ref[...].astype(f32).T.astype(jnp.bfloat16)

    for i in range(BLOCKS_STEP):
        head = lists_smem[0, step * BLOCKS_STEP + i]

        @pl.when(head < 0)
        def _():
            joined[i] = jnp.zeros(joined.shape[1:], joined.dtype)

        @pl.when(head >= 0)
        def _():
            follower = lists_smem[1, head]

            @pl.when(follower < 0)
            def _():
                joined[i] = recv_ref[head]

            @pl.when(follower >= 0)
            def _():
                sums[...] = recv_ref[head].astype(f32)

                def more(s):
                    sums[...] += recv_ref[s].astype(f32)
                    return lists_smem[1, s]

                lax.while_loop(lambda s: s >= 0, more, follower)
                joined[i] = sums[...].astype(joined.dtype)

    for i in range(BLOCKS_STEP):
        swapped = jnp.dot(inner_t[...], joined[i], preferred_element_type=f32)
        out_ref[i] = (swapped + local_ref[i].astype(f32)).astype(out_ref.dtype)


def make_blocks(lists, received, local, basis):
    slots, inner, width = received.shape
    blocks = local.shape[0]
    tiles = pl.BlockSpec((BLOCKS_STEP, width, width), lambda i, s: (i, 0, 0))
    return pl.pallas_call(
        blocks_kernel,
        grid_spec=pltpu.PrefetchScalarGridSpec(
            num_scalar_prefetch=1,
            grid=(blocks // BLOCKS_STEP,),
            in_specs=[
                pl.BlockSpec(received.shape, lambda i, s: (0, 0, 0)),
                pl.BlockSpec((inner, width), lambda i, s: (0, 0)),
                tiles,
            ],
            out_specs=tiles,
            scratch_shapes=[
                pltpu.VMEM((width, inner), jnp.bfloat16),
                pltpu.VMEM((inner, width), jnp.float32),
                pltpu.VMEM((BLOCKS_STEP, inner, width), jnp.bfloat16),
            ],
        ),
        out_shape=jax.ShapeDtypeStruct((blocks, width, width), jnp.bfloat16),
        compiler_params=pltpu.CompilerParams(
            dimension_semantics=("arbitrary",), vmem_limit_bytes=VMEM_BYTES
        ),
        name="make_blocks",
    )(lists, received, basis, local)


def on_device(basis, potentials, orbitals, chan_orbital, pair_list, slot_list, coefs, exchange_ops):
    nrow = lax.axis_size("prow")
    ncol = lax.axis_size("pcol")
    inner, width = exchange_ops.shape[1:]
    received, local, lists = exchange(
        nrow,
        ncol,
        exchange_ops,
        orbitals,
        potentials,
        chan_orbital[None, :],
        slot_list[None, :],
        pair_list.T,
        coefs.T,
        basis,
    )
    blocks = make_blocks(lists, received.reshape(-1, inner, width), local, basis)
    return blocks.reshape(RBLK, 1, BAND, 1, width, width)


def solution(mesh):
    placed = (
        P(),
        P(),
        P("pcol", None),
        P(),
        P(("prow", "pcol"), None),
        P(("prow", "pcol")),
        P(("prow", "pcol"), None),
        P(("prow", "pcol"), None, None),
    )
    return jax.shard_map(
        on_device,
        mesh=mesh,
        in_specs=placed,
        out_specs=P(None, "prow", None, "pcol", None, None),
        check_vma=False,
    )
```

time: 347 us -> 118 us (0.34)
  waiting for transfers between devices: 141 us -> 0 us
  Pallas kernels: 0 us -> 117 us
  matrix products: 77.1 us -> 0 us
  local copies, waits for them, and re-layouts: 56.4 us -> 0 us
  blocking collectives: 31.5 us -> 0 us
  starting transfers between devices: 28.6 us -> 0 us
  other arithmetic: 10.8 us -> 0 us
    all_to_all x6 -> x0, waiting for transfers between devices: 141 us -> none  [the longest x1 91.5 us: on_device(): lax.all_to_all(lax.all_to_all(slot_exchange.reshape(row_devs, col_devs, C...]
    pallas_call x0 -> x2, Pallas kernels: none -> 117 us  [the longest x1 105 us: exchange(): pl.pallas_call(functools.partial(exchange_kernel, nrow, ncol), out_shape=...]
    dot_general x17 -> x0, matrix products: 77.1 us -> none  [the longest x4 50.1 us: sum_blocks(): jnp.dot(select, built_tiles.reshape(built_tiles.shape[0], spline_width *...]
    all_gather x1 -> x0, blocking collectives: 31.5 us -> none  [on_device(): all_orbitals = lax.all_gather(orbitals, 'pcol', axis=0, tiled=True)]
    all_to_all x6 -> x0, starting transfers between devices: 28.6 us -> none  [the longest x1 6 us: on_device(): lax.all_to_all(lax.all_to_all(slot_weight.reshape(row_devs, col_devs, CAP...]
    unnamed x12 -> x0, local copies, waits for them, and re-layouts: 17.2 us -> none
    while x4 -> x0, local copies, waits for them, and re-layouts: 13.4 us -> none
    convert_element_type x5 -> x0, local copies, waits for them, and re-layouts: 12.1 us -> none  [the longest x1 11.6 us: on_device(): blocks.astype(jnp.bfloat16)]
  transfers between devices with their start and end apart: 6 -> 0, of which waited for: 3 -> 0; matrix products, arithmetic and copies ran while one was open for 10% -> 0% of each run, Pallas kernels for 0% -> 0%
where the time goes in v2:
time: 118 us; the launch traced here: 117 us
  Pallas kernels  117 us (99%)
    pallas_call x1, Pallas kernels, exchange(): pl.pallas_call(functools.partial(exchange_kernel, nrow, ncol), out_shape=...  105 us
    pallas_call x1, Pallas kernels, make_blocks(): pl.pallas_call(blocks_kernel, grid_spec=pltpu.PrefetchScalarGridSpec(num_...  12.6 us

profile of v2, /device:TPU:0, one launch (start us, length us, event | category | flops | bytes accessed | tf_op | source)
XLA Modules:
  0.0 117.2 jit_solution(7753603404872681441)
XLA Ops:
  0.0 104.6 %exchange.1 = (bf16[32,2,128,256]{3,2,1,0:T(8,128)(2,1)}, bf16[64,256,256]{2,1,0:T(8,128)(2,1)}, s32[8,128]{1,0:T(8,128)}) custom-call(bf16[192,128,256]{2,1,0:T(8,128)(2,1)} %ops_ref.1, bf16[8,512]{1,0:T(8,128)(2,1)} %orb_ref.1, f32[8,512]{1,0:T(8,128)} %pot_ref.1, s32[1,128]{1,0:T(1,128)} %bitcast.12, s32[1,192]{1,0:T(1,128)} %bitcast.11, ...), custom_call_target="tpu_custom_call" | custom-call | tf_op jit(solution)/shard_map/exchange/pallas_call | solution.py:323
  104.6 12.6 %make_blocks.1 = bf16[64,256,256]{2,1,0:T(8,128)(2,1)} custom-call(s32[8,128]{1,0:T(8,128)} %get-tuple-element.8.lists_smem, bf16[64,128,256]{2,1,0:T(8,128)(2,1)} %bitcast.8, bf16[512,256]{1,0:T(8,128)(2,1)} %inner_ref.1, bf16[64,256,256]{2,1,0:T(8,128)(2,1)} %get-tuple-element.10.local_ref), custom_call_target="tpu_custom_call" | custom-call | tf_op jit(solution)/shard_map/make_blocks/pallas_call | solution.py:407

commit v3 on v2

--- a/solution.py
+++ b/solution.py
@@ -13,7 +13,9 @@
 BLOCKS_STEP = 8
 FIRST_ROWS = 32
 SPAN = 16
-VMEM_BYTES = 56 * 1024 * 1024
+NEAR_BYTES = 8 * 1024 * 1024
+EXCHANGE_BYTES = 48 * 1024 * 1024
+BLOCKS_BYTES = 40 * 1024 * 1024
 MESH = pl.DeviceIdType.MESH
 EXACT = lax.Precision.HIGHEST
 FAR = 1.0e6
@@ -31,6 +33,14 @@
 
 def iota(shape, dim):
     return lax.broadcasted_iota(jnp.int32, shape, dim)
+
+
+def masked(index, mask, count):
+    flipped = 0
+    for b in range(count.bit_length() - 1):
+        bits = lax.div(index, 2**b) + lax.div(mask, 2**b)
+        flipped = flipped + lax.rem(bits, 2) * 2**b
+    return flipped
 
 
 def turned(row):
@@ -84,7 +94,6 @@
     pot_pad,
     basis_t,
     weights,
-    local_blocks,
     table,
     order_smem,
     orb_ssem,
@@ -113,9 +122,14 @@
     chunks = ((terms_a, send_a, 0), (terms_b, send_b, FIRST_ROWS))
 
     def peer(t):
-        dq = lax.rem(t * (ncol // 2 + 1), ncol)
-        dp = lax.rem(lax.div(t, ncol) + t, nrow)
-        return lax.rem(p + dp, nrow), lax.rem(q + dq, ncol)
+        low = lax.rem(t, ncol)
+        mask = 0
+        for b in range(ncol.bit_length() - 1):
+            mask = mask * 2 + lax.rem(lax.div(low, 2**b), 2)
+        return (
+            masked(p, lax.rem(lax.div(t, ncol) + t, nrow), nrow),
+            masked(q, mask, ncol),
+        )
 
     def each(count, action):
         def body(t, c):
@@ -293,18 +307,15 @@
 
     def form(t, carried):
         scaled = (basis_t[...] * weights[pl.ds(t, 1), :]).astype(bf16)
-        local_blocks[t] = jnp.dot(
+        local_ref[t] = jnp.dot(
             scaled, basis_ref[...], preferred_element_type=f32
         ).astype(bf16)
         return carried
 
     lax.fori_loop(0, blocks, form, 0)
-    out_copy = pltpu.make_async_copy(local_blocks, local_ref, own_sem.at[5])
-    out_copy.start()
     for c in range(len(chunks)):
         each(ndev, lambda t: exch_copy(c, t).wait())
         own_copy(c).wait()
-    out_copy.wait()
 
 
 def exchange(nrow, ncol, exchange_ops, orbitals, potentials, chan, slot, pairs, coefs, basis):
@@ -316,6 +327,8 @@
     size = -(-max(ndev * CAP, 128) // 128) * 128
     span = -(-max(ndev * CAP, terms) // 128) * 128
     rest = inner - FIRST_ROWS
+    near = ndev * CAP * inner * width * 2 <= NEAR_BYTES
+    place = pltpu.VMEM if near else jax.ShapeDtypeStruct
     any_spec = pl.BlockSpec(memory_space=pl.ANY)
     vmem = pl.BlockSpec(memory_space=pltpu.VMEM)
     dma = pltpu.SemaphoreType.DMA
@@ -323,12 +336,12 @@
     return pl.pallas_call(
         functools.partial(exchange_kernel, nrow, ncol),
         out_shape=(
-            jax.ShapeDtypeStruct((ndev, CAP, inner, width), bf16),
-            jax.ShapeDtypeStruct((blocks, width, width), bf16),
-            jax.ShapeDtypeStruct((8, size), jnp.int32),
+            place((ndev, CAP, inner, width), bf16),
+            pltpu.VMEM((blocks, width, width), bf16),
+            pltpu.VMEM((8, size), jnp.int32),
         ),
         in_specs=[any_spec] + [vmem] * 7,
-        out_specs=(any_spec, any_spec, vmem),
+        out_specs=(vmem if near else any_spec, vmem, vmem),
         scratch_shapes=[
             pltpu.VMEM((terms, FIRST_ROWS, width), bf16),
             pltpu.VMEM((terms, rest, width), bf16),
@@ -343,7 +356,6 @@
             pltpu.VMEM((128, points), f32),
             pltpu.VMEM((width, points), f32),
             pltpu.VMEM((128, points), f32),
-            pltpu.VMEM((blocks, width, width), bf16),
             pltpu.VMEM((8, span), jnp.int32),
             pltpu.SMEM((8, span), jnp.int32),
             dma((ncol,)),
@@ -352,79 +364,116 @@
             dma((ndev,)),
             dma((2, ndev)),
             dma((2, ndev)),
-            dma((6,)),
+            dma((5,)),
         ],
         compiler_params=pltpu.CompilerParams(
-            collective_id=0, has_side_effects=True, vmem_limit_bytes=VMEM_BYTES
+            collective_id=0, has_side_effects=True, vmem_limit_bytes=EXCHANGE_BYTES
         ),
         name="exchange",
     )(exchange_ops, orbitals, potentials, chan, slot, pairs, coefs, basis)
 
 
-def blocks_kernel(lists_smem, recv_ref, inner_ref, local_ref, out_ref, inner_t, sums, joined):
-    step = pl.program_id(0)
+def blocks_kernel(
+    lists_ref,
+    recv_ref,
+    basis_ref,
+    local_ref,
+    out_ref,
+    lists_smem,
+    inner_t,
+    sums,
+    joined,
+    formed,
+    sems,
+    lists_sem,
+):
     f32 = jnp.float32
-
-    @pl.when(step == 0)
-    def _():
-        inner_t[...] = inner_ref[...].astype(f32).T.astype(jnp.bfloat16)
-
-    for i in range(BLOCKS_STEP):
-        head = lists_smem[0, step * BLOCKS_STEP + i]
-
-        @pl.when(head < 0)
+    steps = local_ref.shape[0] // BLOCKS_STEP
+    lists_copy = pltpu.make_async_copy(lists_ref, lists_smem, lists_sem)
+    lists_copy.start()
+    inner_t[...] = basis_ref[: recv_ref.shape[1], :].astype(f32).T.astype(jnp.bfloat16)
+
+    def leave(step):
+        span = pl.ds(step * BLOCKS_STEP, BLOCKS_STEP)
+        return pltpu.make_async_copy(formed.at[span], out_ref.at[span], sems.at[step])
+
+    def work(step, carried):
+        longest = jnp.int32(-1)
+        for i in range(BLOCKS_STEP):
+            head = lists_smem[0, step * BLOCKS_STEP + i]
+            follower = jnp.where(head < 0, -1, lists_smem[1, jnp.maximum(head, 0)])
+            third = jnp.where(follower < 0, -1, lists_smem[1, jnp.maximum(follower, 0)])
+            longest = jnp.maximum(longest, third)
+            one = recv_ref[jnp.maximum(head, 0)].astype(f32)
+            two = recv_ref[jnp.maximum(follower, 0)].astype(f32)
+            nothing = jnp.zeros_like(one)
+            joined[i] = (
+                jnp.where(head < 0, nothing, one) + jnp.where(follower < 0, nothing, two)
+            ).astype(joined.dtype)
+
+        @pl.when(longest >= 0)
         def _():
-            joined[i] = jnp.zeros(joined.shape[1:], joined.dtype)
-
-        @pl.when(head >= 0)
-        def _():
-            follower = lists_smem[1, head]
-
-            @pl.when(follower < 0)
-            def _():
-                joined[i] = recv_ref[head]
-
-            @pl.when(follower >= 0)
-            def _():
-                sums[...] = recv_ref[head].astype(f32)
-
-                def more(s):
-                    sums[...] += recv_ref[s].astype(f32)
-                    return lists_smem[1, s]
-
-                lax.while_loop(lambda s: s >= 0, more, follower)
-                joined[i] = sums[...].astype(joined.dtype)
-
-    for i in range(BLOCKS_STEP):
-        swapped = jnp.dot(inner_t[...], joined[i], preferred_element_type=f32)
-        out_ref[i] = (swapped + local_ref[i].astype(f32)).astype(out_ref.dtype)
+            def rejoin(i, c):
+                head = lists_smem[0, step * BLOCKS_STEP + i]
+                follower = jnp.where(head < 0, -1, lists_smem[1, jnp.maximum(head, 0)])
+                third = jnp.where(follower < 0, -1, lists_smem[1, jnp.maximum(follower, 0)])
+
+                @pl.when(third >= 0)
+                def _():
+                    sums[...] = recv_ref[head].astype(f32) + recv_ref[follower].astype(f32)
+
+                    def more(s):
+                        sums[...] += recv_ref[s].astype(f32)
+                        return lists_smem[1, s]
+
+                    lax.while_loop(lambda s: s >= 0, more, third)
+                    joined[i] = sums[...].astype(joined.dtype)
+
+                return c
+
+            lax.fori_loop(0, BLOCKS_STEP, rejoin, 0)
+
+        for i in range(BLOCKS_STEP):
+            t = step * BLOCKS_STEP + i
+            swapped = jnp.dot(inner_t[...], joined[i], preferred_element_type=f32)
+            formed[t] = (swapped + local_ref[t].astype(f32)).astype(formed.dtype)
+        leave(step).start()
+        return carried
+
+    lists_copy.wait()
+    lax.fori_loop(0, steps, work, 0)
+
+    def finish(step, carried):
+        leave(step).wait()
+        return carried
+
+    lax.fori_loop(0, steps, finish, 0)
 
 
 def make_blocks(lists, received, local, basis):
     slots, inner, width = received.shape
     blocks = local.shape[0]
-    tiles = pl.BlockSpec((BLOCKS_STEP, width, width), lambda i, s: (i, 0, 0))
+    vmem = pl.BlockSpec(memory_space=pltpu.VMEM)
     return pl.pallas_call(
         blocks_kernel,
-        grid_spec=pltpu.PrefetchScalarGridSpec(
-            num_scalar_prefetch=1,
-            grid=(blocks // BLOCKS_STEP,),
-            in_specs=[
-                pl.BlockSpec(received.shape, lambda i, s: (0, 0, 0)),
-                pl.BlockSpec((inner, width), lambda i, s: (0, 0)),
-                tiles,
-            ],
-            out_specs=tiles,
-            scratch_shapes=[
-                pltpu.VMEM((width, inner), jnp.bfloat16),
-                pltpu.VMEM((inner, width), jnp.float32),
-                pltpu.VMEM((BLOCKS_STEP, inner, width), jnp.bfloat16),
-            ],
-        ),
+        in_specs=[
+            vmem,
+            vmem,
+            vmem,
+            vmem,
+        ],
+        out_specs=pl.BlockSpec(memory_space=pl.ANY),
+        scratch_shapes=[
+            pltpu.SMEM(lists.shape, jnp.int32),
+            pltpu.VMEM((width, inner), jnp.bfloat16),
+            pltpu.VMEM((inner, width), jnp.float32),
+            pltpu.VMEM((BLOCKS_STEP, inner, width), jnp.bfloat16),
+            pltpu.VMEM((blocks, width, width), jnp.bfloat16),
+            pltpu.SemaphoreType.DMA((blocks // BLOCKS_STEP,)),
+            pltpu.SemaphoreType.DMA,
+        ],
         out_shape=jax.ShapeDtypeStruct((blocks, width, width), jnp.bfloat16),
-        compiler_params=pltpu.CompilerParams(
-            dimension_semantics=("arbitrary",), vmem_limit_bytes=VMEM_BYTES
-        ),
+        compiler_params=pltpu.CompilerParams(vmem_limit_bytes=BLOCKS_BYTES),
         name="make_blocks",
     )(lists, received, basis, local)
 

time: 118 us -> 122 us (1.034)
  local copies, waits for them, and re-layouts: 0 us -> 10.9 us
  Pallas kernels: 117 us -> 110 us
    unnamed x0 -> x10, local copies, waits for them, and re-layouts: none -> 10.9 us
    pallas_call x1, Pallas kernels: 12.6 us -> 7.36 us  [make_blocks(): pl.pallas_call(blocks_kernel, in_specs=[vmem, vmem, vmem, vmem], out_spec...]
    pallas_call x1, Pallas kernels: 105 us -> 103 us  [exchange(): pl.pallas_call(functools.partial(exchange_kernel, nrow, ncol), out_shape=...]
where the time goes in v3:
time: 122 us; the launch traced here: 121 us
  Pallas kernels  110 us (90%)
  local copies, waits for them, and re-layouts  10.9 us (9%)
    pallas_call x1, Pallas kernels, exchange(): pl.pallas_call(functools.partial(exchange_kernel, nrow, ncol), out_shape=...  103 us
    unnamed x10, local copies, waits for them, and re-layouts  10.9 us
    pallas_call x1, Pallas kernels, make_blocks(): pl.pallas_call(blocks_kernel, in_specs=[vmem, vmem, vmem, vmem], out_spec...  7.36 us

profile of v3, /device:TPU:0, one launch (start us, length us, event | category | flops | bytes accessed | tf_op | source)
XLA Modules:
  0.0 121.3 jit_solution(7938171340594555976)
XLA Ops:
  0.0 0.0 copy-start.4
  0.0 103.0 %exchange.1 = (bf16[32,2,128,256]{3,2,1,0:T(8,128)(2,1)S(1)}, bf16[64,256,256]{2,1,0:T(8,128)(2,1)S(1)}, s32[8,128]{1,0:T(8,128)S(1)}) custom-call(bf16[192,128,256]{2,1,0:T(8,128)(2,1)} %ops_ref.1, bf16[8,512]{1,0:T(8,128)(2,1)} %orb_ref.1, f32[8,512]{1,0:T(8,128)} %pot_ref.1, s32[1,128]{1,0:T(1,128)} %bitcast.12, s32[1,192]{1,0:T(1,128)} %bitcast.11, ...), custom_call_target="tpu_custom_call" | custom-call | tf_op jit(solution)/shard_map/exchange/pallas_call | solution.py:336
  103.0 0.0 copy-start
  103.0 3.4 %copy-done = bf16[64,256,256]{2,1,0:T(8,128)(2,1)} copy-done((bf16[64,256,256]{2,1,0:T(8,128)(2,1)}, bf16[64,256,256]{2,1,0:T(8,128)(2,1)S(1)}, u32[]{:S(2)}) %copy-start) | copy-done | bytes 8388632
  106.4 0.0 copy-start.2
  106.4 1.9 %copy-done.2 = bf16[32,2,128,256]{3,2,1,0:T(8,128)(2,1)} copy-done((bf16[32,2,128,256]{3,2,1,0:T(8,128)(2,1)}, bf16[32,2,128,256]{3,2,1,0:T(8,128)(2,1)S(1)}, u32[]{:S(2)}) %copy-start.2) | copy-done | bytes 4194328
  108.3 0.0 copy-done.4
  108.3 0.0 copy-start.1
  108.3 3.4 %copy-done.1 = bf16[64,256,256]{2,1,0:T(8,128)(2,1)S(1)} copy-done((bf16[64,256,256]{2,1,0:T(8,128)(2,1)S(1)}, bf16[64,256,256]{2,1,0:T(8,128)(2,1)}, u32[]{:S(2)}) %copy-start.1) | copy-done | bytes 8388632
  111.7 0.0 copy-start.3
  111.7 2.2 %copy-done.3 = bf16[32,2,128,256]{3,2,1,0:T(8,128)(2,1)S(1)} copy-done((bf16[32,2,128,256]{3,2,1,0:T(8,128)(2,1)S(1)}, bf16[32,2,128,256]{3,2,1,0:T(8,128)(2,1)}, u32[]{:S(2)}) %copy-start.3) | copy-done | bytes 4194328
  113.9 7.4 %make_blocks.1 = bf16[64,256,256]{2,1,0:T(8,128)(2,1)} custom-call(s32[8,128]{1,0:T(8,128)S(1)} %get-tuple-element.8.lists_ref, bf16[64,128,256]{2,1,0:T(8,128)(2,1)S(1)} %bitcast.8, bf16[512,256]{1,0:T(8,128)(2,1)S(1)} %copy-done.4, bf16[64,256,256]{2,1,0:T(8,128)(2,1)S(1)} %copy-done.1), custom_call_target="tpu_custom_call" | custom-call | tf_op jit(solution)/shard_map/make_blocks/pallas_call | solution.py:457
Async XLA Ops:
  0.0 108.3 %copy-start.4 = (bf16[512,256]{1,0:T(8,128)(2,1)S(1)}, bf16[512,256]{1,0:T(8,128)(2,1)}, u32[]{:S(2)}) copy-start(bf16[512,256]{1,0:T(8,128)(2,1)} %basis_ref.3) | copy-start | bytes 786436
  103.0 3.4 %copy-start = (bf16[64,256,256]{2,1,0:T(8,128)(2,1)}, bf16[64,256,256]{2,1,0:T(8,128)(2,1)S(1)}, u32[]{:S(2)}) copy-start(bf16[64,256,256]{2,1,0:T(8,128)(2,1)S(1)} %get-tuple-element.10.local_ref) | copy-start | bytes 25165828
  106.4 1.9 %copy-start.2 = (bf16[32,2,128,256]{3,2,1,0:T(8,128)(2,1)}, bf16[32,2,128,256]{3,2,1,0:T(8,128)(2,1)S(1)}, u32[]{:S(2)}) copy-start(bf16[32,2,128,256]{3,2,1,0:T(8,128)(2,1)S(1)} %get-tuple-element.9) | copy-start | bytes 12582916
  108.3 3.4 %copy-start.1 = (bf16[64,256,256]{2,1,0:T(8,128)(2,1)S(1)}, bf16[64,256,256]{2,1,0:T(8,128)(2,1)}, u32[]{:S(2)}) copy-start(bf16[64,256,256]{2,1,0:T(8,128)(2,1)} %copy-done) | copy-start | bytes 25165828
  111.7 2.2 %copy-start.3 = (bf16[32,2,128,256]{3,2,1,0:T(8,128)(2,1)S(1)}, bf16[32,2,128,256]{3,2,1,0:T(8,128)(2,1)}, u32[]{:S(2)}) copy-start(bf16[32,2,128,256]{3,2,1,0:T(8,128)(2,1)} %copy-done.2) | copy-start | bytes 12582916

commit v4 on v3

--- a/solution.py
+++ b/solution.py
@@ -11,7 +11,7 @@
 BAND = 2
 RBLK = 32
 BLOCKS_STEP = 8
-FIRST_ROWS = 32
+FIRST_ROWS = 16
 SPAN = 16
 NEAR_BYTES = 8 * 1024 * 1024
 EXCHANGE_BYTES = 48 * 1024 * 1024
@@ -190,13 +190,44 @@
         lambda t: pl.semaphore_signal(barrier, inc=1, device_id=peer(t), device_id_type=MESH),
     )
 
+    slot = slot_ref[...]
+    slot_order(slot, slots, table)
+    order_copy = pltpu.make_async_copy(table, order_smem, own_sem.at[4])
+    order_copy.start()
+    order_copy.wait()
+
+    def add_slots(c):
+        buffer, send, _ = chunks[c]
+        height, width = buffer.shape[1:]
+        load(c).wait()
+
+        def add(i, total):
+            kept = jnp.where(order_smem[1, i] > 0, total, jnp.zeros_like(total))
+            total = kept + buffer[jnp.clip(order_smem[0, i], 0, top)].astype(f32)
+            running[i, :height, :] = total.astype(bf16)
+            return total
+
+        lax.fori_loop(0, terms, add, jnp.zeros((height, width), f32), unroll=4)
+
+        def place(o, carried):
+            for k in range(CAP):
+                end = jnp.clip(order_smem[2, o * CAP + k], 0, top)
+                send[o, k] = running[end, :height, :]
+            return carried
+
+        lax.fori_loop(0, ndev, place, 0)
+
+    add_slots(0)
+    pl.semaphore_wait(barrier, ndev - 1)
+    each(ndev, lambda t: exch_copy(0, t).start())
+    own_copy(0).start()
+
     orb_wide[...] = jnp.zeros_like(orb_wide)
     orb_wide[:orb_per, :] = orb_ref[...].astype(f32)
     orb_send[...] = jnp.concatenate(
         [orb_wide[:, : points // 2], orb_wide[:, points // 2 :]], axis=0
     ).astype(bf16)
 
-    slot = slot_ref[...]
     first, second, multipole = pair_ref[0:1, :], pair_ref[1:2, :], pair_ref[2:3, :]
     offset = (second // ncol - first // ncol + groups) % groups
     block = (first // nrow * BAND + offset).astype(f32)
@@ -213,35 +244,12 @@
         message = jnp.where(lane == base + 9, number, message)
     msg_send[...] = message.reshape(ndev, 1, 128)
 
-    slot_order(slot, slots, table)
-    order_copy = pltpu.make_async_copy(table, order_smem, own_sem.at[4])
-    order_copy.start()
-    pl.semaphore_wait(barrier, ndev - 1)
     each(ncol, lambda t: orb_copy(t).start())
     each(ndev, lambda t: msg_copy(t).start())
-    order_copy.wait()
-
-    for c, (buffer, send, _) in enumerate(chunks):
-        height, width = buffer.shape[1:]
-        load(c).wait()
-
-        def add(i, total):
-            kept = jnp.where(order_smem[1, i] > 0, total, jnp.zeros_like(total))
-            total = kept + buffer[jnp.clip(order_smem[0, i], 0, top)].astype(f32)
-            running[i, :height, :] = total.astype(bf16)
-            return total
-
-        lax.fori_loop(0, terms, add, jnp.zeros((height, width), f32), unroll=4)
-
-        def place(o, carried):
-            for k in range(CAP):
-                end = jnp.clip(order_smem[2, o * CAP + k], 0, top)
-                send[o, k] = running[end, :height, :]
-            return carried
-
-        lax.fori_loop(0, ndev, place, 0)
-        each(ndev, lambda t: exch_copy(c, t).start())
-        own_copy(c).start()
+
+    add_slots(1)
+    each(ndev, lambda t: exch_copy(1, t).start())
+    own_copy(1).start()
 
     each(ncol, lambda t: orb_copy(t).wait())
     all_orb[q] = orb_send[...]
@@ -338,7 +346,7 @@
         out_shape=(
             place((ndev, CAP, inner, width), bf16),
             pltpu.VMEM((blocks, width, width), bf16),
-            pltpu.VMEM((8, size), jnp.int32),
+            jax.ShapeDtypeStruct((8, size), jnp.int32),
         ),
         in_specs=[any_spec] + [vmem] * 7,
         out_specs=(vmem if near else any_spec, vmem, vmem),
@@ -382,7 +390,8 @@
     lists_smem,
     inner_t,
     sums,
-    joined,
+    joined_a,
+    joined_b,
     formed,
     sems,
     lists_sem,
@@ -397,26 +406,32 @@
         span = pl.ds(step * BLOCKS_STEP, BLOCKS_STEP)
         return pltpu.make_async_copy(formed.at[span], out_ref.at[span], sems.at[step])
 
-    def work(step, carried):
-        longest = jnp.int32(-1)
-        for i in range(BLOCKS_STEP):
-            head = lists_smem[0, step * BLOCKS_STEP + i]
-            follower = jnp.where(head < 0, -1, lists_smem[1, jnp.maximum(head, 0)])
-            third = jnp.where(follower < 0, -1, lists_smem[1, jnp.maximum(follower, 0)])
-            longest = jnp.maximum(longest, third)
-            one = recv_ref[jnp.maximum(head, 0)].astype(f32)
-            two = recv_ref[jnp.maximum(follower, 0)].astype(f32)
-            nothing = jnp.zeros_like(one)
-            joined[i] = (
-                jnp.where(head < 0, nothing, one) + jnp.where(follower < 0, nothing, two)
-            ).astype(joined.dtype)
-
+    def slots_of(step, i):
+        head = lists_smem[0, step * BLOCKS_STEP + i]
+        follower = jnp.where(head < 0, -1, lists_smem[1, jnp.maximum(head, 0)])
+        third = jnp.where(follower < 0, -1, lists_smem[1, jnp.maximum(follower, 0)])
+        return head, follower, third
+
+    def join(step, joined, i):
+        head, follower, third = slots_of(step, i)
+        one = recv_ref[jnp.maximum(head, 0)].astype(f32)
+        two = recv_ref[jnp.maximum(follower, 0)].astype(f32)
+        nothing = jnp.zeros_like(one)
+        joined[i] = (
+            jnp.where(head < 0, nothing, one) + jnp.where(follower < 0, nothing, two)
+        ).astype(joined.dtype)
+        return third
+
+    def multiply(step, joined, i):
+        t = step * BLOCKS_STEP + i
+        swapped = jnp.dot(inner_t[...], joined[i], preferred_element_type=f32)
+        formed[t] = (swapped + local_ref[t].astype(f32)).astype(formed.dtype)
+
+    def join_long(step, joined, longest):
         @pl.when(longest >= 0)
         def _():
             def rejoin(i, c):
-                head = lists_smem[0, step * BLOCKS_STEP + i]
-                follower = jnp.where(head < 0, -1, lists_smem[1, jnp.maximum(head, 0)])
-                third = jnp.where(follower < 0, -1, lists_smem[1, jnp.maximum(follower, 0)])
+                head, follower, third = slots_of(step, i)
 
                 @pl.when(third >= 0)
                 def _():
@@ -424,7 +439,8 @@
 
                     def more(s):
                         sums[...] += recv_ref[s].astype(f32)
-                        return lists_smem[1, s]
+                        after = lists_smem[1, s]
+                        return jnp.where(after > s, after, -1)
 
                     lax.while_loop(lambda s: s >= 0, more, third)
                     joined[i] = sums[...].astype(joined.dtype)
@@ -433,15 +449,26 @@
 
             lax.fori_loop(0, BLOCKS_STEP, rejoin, 0)
 
+    def work(step, now, later):
+        following = jnp.minimum(step + 1, steps - 1)
+        longest = jnp.int32(-1)
         for i in range(BLOCKS_STEP):
-            t = step * BLOCKS_STEP + i
-            swapped = jnp.dot(inner_t[...], joined[i], preferred_element_type=f32)
-            formed[t] = (swapped + local_ref[t].astype(f32)).astype(formed.dtype)
+            multiply(step, now, i)
+            longest = jnp.maximum(longest, join(following, later, i))
         leave(step).start()
+        join_long(following, later, longest)
+
+    def work_pair(pair, carried):
+        work(2 * pair, joined_a, joined_b)
+        work(2 * pair + 1, joined_b, joined_a)
         return carried
 
     lists_copy.wait()
-    lax.fori_loop(0, steps, work, 0)
+    longest = jnp.int32(-1)
+    for i in range(BLOCKS_STEP):
+        longest = jnp.maximum(longest, join(0, joined_a, i))
+    join_long(0, joined_a, longest)
+    lax.fori_loop(0, steps // 2, work_pair, 0)
 
     def finish(step, carried):
         leave(step).wait()
@@ -457,7 +484,7 @@
     return pl.pallas_call(
         blocks_kernel,
         in_specs=[
-            vmem,
+            pl.BlockSpec(memory_space=pl.ANY),
             vmem,
             vmem,
             vmem,
@@ -467,6 +494,7 @@
             pltpu.SMEM(lists.shape, jnp.int32),
             pltpu.VMEM((width, inner), jnp.bfloat16),
             pltpu.VMEM((inner, width), jnp.float32),
+            pltpu.VMEM((BLOCKS_STEP, inner, width), jnp.bfloat16),
             pltpu.VMEM((BLOCKS_STEP, inner, width), jnp.bfloat16),
             pltpu.VMEM((blocks, width, width), jnp.bfloat16),
             pltpu.SemaphoreType.DMA((blocks // BLOCKS_STEP,)),

time: 122 us -> 113 us (0.926)
  local copies, waits for them, and re-layouts: 10.9 us -> 0.68 us
    unnamed x10 -> x4, local copies, waits for them, and re-layouts: 10.9 us -> 0.68 us
where the time goes in v4:
time: 113 us; the launch traced here: 112 us
  Pallas kernels  111 us (98%)
    pallas_call x1, Pallas kernels, exchange(): pl.pallas_call(functools.partial(exchange_kernel, nrow, ncol), out_shape=...  104 us
    pallas_call x1, Pallas kernels, make_blocks(): pl.pallas_call(blocks_kernel, in_specs=[pl.BlockSpec(memory_space=pl.ANY)...  7.24 us

profile of v4, /device:TPU:0, one launch (start us, length us, event | category | flops | bytes accessed | tf_op | source)
XLA Modules:
  0.0 112.0 jit_solution(1339991395834738745)
XLA Ops:
  0.0 0.0 copy-start
  0.0 104.0 %exchange.1 = (bf16[32,2,128,256]{3,2,1,0:T(8,128)(2,1)S(1)}, bf16[64,256,256]{2,1,0:T(8,128)(2,1)S(1)}, s32[8,128]{1,0:T(8,128)}) custom-call(bf16[192,128,256]{2,1,0:T(8,128)(2,1)} %ops_ref.1, bf16[8,512]{1,0:T(8,128)(2,1)} %orb_ref.1, f32[8,512]{1,0:T(8,128)} %pot_ref.1, s32[1,128]{1,0:T(1,128)} %bitcast.12, s32[1,192]{1,0:T(1,128)} %bitcast.11, ...), custom_call_target="tpu_custom_call" | custom-call | tf_op jit(solution)/shard_map/exchange/pallas_call | solution.py:344
  104.0 0.0 copy-done
  104.0 0.0 copy-start.1
  104.1 0.7 copy-done.1
  104.7 7.2 %make_blocks.1 = bf16[64,256,256]{2,1,0:T(8,128)(2,1)} custom-call(s32[8,128]{1,0:T(8,128)S(1)} %copy-done.1, bf16[64,128,256]{2,1,0:T(8,128)(2,1)S(1)} %bitcast.8, bf16[512,256]{1,0:T(8,128)(2,1)S(1)} %copy-done, bf16[64,256,256]{2,1,0:T(8,128)(2,1)S(1)} %get-tuple-element.10.local_ref), custom_call_target="tpu_custom_call" | custom-call | tf_op jit(solution)/shard_map/make_blocks/pallas_call | solution.py:484
Async XLA Ops:
  0.0 104.0 %copy-start = (bf16[512,256]{1,0:T(8,128)(2,1)S(1)}, bf16[512,256]{1,0:T(8,128)(2,1)}, u32[]{:S(2)}) copy-start(bf16[512,256]{1,0:T(8,128)(2,1)} %basis_ref.3) | copy-start | bytes 786436
  104.0 0.7 copy-start.1

commit v5 on v4

--- a/solution.py
+++ b/solution.py
@@ -11,7 +11,7 @@
 BAND = 2
 RBLK = 32
 BLOCKS_STEP = 8
-FIRST_ROWS = 16
+BANDS = (16, 32)
 SPAN = 16
 NEAR_BYTES = 8 * 1024 * 1024
 EXCHANGE_BYTES = 48 * 1024 * 1024
@@ -83,9 +83,12 @@
     lists_ref,
     terms_a,
     terms_b,
+    terms_c,
     running,
     send_a,
     send_b,
+    send_c,
+    lists,
     orb_wide,
     orb_send,
     all_orb,
@@ -119,7 +122,11 @@
     orb_per = orb_ref.shape[0]
     orb_rows = orb_wide.shape[0]
     top = terms - 1
-    chunks = ((terms_a, send_a, 0), (terms_b, send_b, FIRST_ROWS))
+    chunks = (
+        (terms_a, send_a, 0),
+        (terms_b, send_b, BANDS[0]),
+        (terms_c, send_c, BANDS[0] + BANDS[1]),
+    )
 
     def peer(t):
         low = lax.rem(t, ncol)
@@ -180,10 +187,10 @@
         )
 
     def own_copy(c):
-        return pltpu.make_async_copy(chunks[c][1].at[me], landing(c), own_sem.at[2 + c])
-
-    load(0).start()
-    load(1).start()
+        return pltpu.make_async_copy(chunks[c][1].at[me], landing(c), own_sem.at[3 + c])
+
+    for c in range(len(chunks)):
+        load(c).start()
     barrier = pltpu.get_barrier_semaphore()
     each(
         ndev,
@@ -192,7 +199,7 @@
 
     slot = slot_ref[...]
     slot_order(slot, slots, table)
-    order_copy = pltpu.make_async_copy(table, order_smem, own_sem.at[4])
+    order_copy = pltpu.make_async_copy(table, order_smem, own_sem.at[6])
     order_copy.start()
     order_copy.wait()
 
@@ -247,9 +254,10 @@
     each(ncol, lambda t: orb_copy(t).start())
     each(ndev, lambda t: msg_copy(t).start())
 
-    add_slots(1)
-    each(ndev, lambda t: exch_copy(1, t).start())
-    own_copy(1).start()
+    for c in range(1, len(chunks)):
+        add_slots(c)
+        each(ndev, lambda t: exch_copy(c, t).start())
+        own_copy(c).start()
 
     each(ncol, lambda t: orb_copy(t).wait())
     all_orb[q] = orb_send[...]
@@ -294,7 +302,7 @@
         orbital_of(first_chan) * orbital_of(second_chan)
     )
 
-    size = lists_ref.shape[1]
+    size = lists.shape[1]
     source = iota((ndev, size), 0)
     spot = iota((ndev, size), 1)
     row = jnp.full((1, size), -1.0, f32)
@@ -307,10 +315,12 @@
     over = iota((size, size), 1).astype(f32)
     heads = jnp.min(jnp.where(col == over, under, FAR), axis=0, keepdims=True)
     nexts = jnp.min(jnp.where((col == row) & (under > over), under, FAR), axis=0, keepdims=True)
-    lists_ref[...] = jnp.zeros_like(lists_ref)
-    lists_ref[0:1, :] = jnp.where(heads < FAR, heads, -1.0).astype(jnp.int32)
-    lists_ref[1:2, :] = jnp.where(nexts < FAR, nexts, -1.0).astype(jnp.int32)
-
+    lists[...] = jnp.zeros_like(lists)
+    lists[0:1, :] = jnp.where(heads < FAR, heads, -1.0).astype(jnp.int32)
+    lists[1:2, :] = jnp.where(nexts < FAR, nexts, -1.0).astype(jnp.int32)
+
+    lists_copy = pltpu.make_async_copy(lists, lists_ref, own_sem.at[7])
+    lists_copy.start()
     basis_t[...] = basis_ref[...].astype(f32).T
 
     def form(t, carried):
@@ -324,6 +334,7 @@
     for c in range(len(chunks)):
         each(ndev, lambda t: exch_copy(c, t).wait())
         own_copy(c).wait()
+    lists_copy.wait()
 
 
 def exchange(nrow, ncol, exchange_ops, orbitals, potentials, chan, slot, pairs, coefs, basis):
@@ -334,10 +345,11 @@
     orb_rows = -(-orbitals.shape[0] // 8) * 8
     size = -(-max(ndev * CAP, 128) // 128) * 128
     span = -(-max(ndev * CAP, terms) // 128) * 128
-    rest = inner - FIRST_ROWS
+    heights = BANDS + (inner - sum(BANDS),)
     near = ndev * CAP * inner * width * 2 <= NEAR_BYTES
     place = pltpu.VMEM if near else jax.ShapeDtypeStruct
     any_spec = pl.BlockSpec(memory_space=pl.ANY)
+    smem = pl.BlockSpec(memory_space=pltpu.SMEM)
     vmem = pl.BlockSpec(memory_space=pltpu.VMEM)
     dma = pltpu.SemaphoreType.DMA
     f32, bf16 = jnp.float32, jnp.bfloat16
@@ -346,16 +358,15 @@
         out_shape=(
             place((ndev, CAP, inner, width), bf16),
             pltpu.VMEM((blocks, width, width), bf16),
-            jax.ShapeDtypeStruct((8, size), jnp.int32),
+            pltpu.SMEM((8, size), jnp.int32),
         ),
         in_specs=[any_spec] + [vmem] * 7,
-        out_specs=(vmem if near else any_spec, vmem, vmem),
+        out_specs=(vmem if near else any_spec, vmem, smem),
         scratch_shapes=[
-            pltpu.VMEM((terms, FIRST_ROWS, width), bf16),
-            pltpu.VMEM((terms, rest, width), bf16),
-            pltpu.VMEM((terms, max(rest, FIRST_ROWS), width), bf16),
-            pltpu.VMEM((ndev, CAP, FIRST_ROWS, width), bf16),
-            pltpu.VMEM((ndev, CAP, rest, width), bf16),
+            *[pltpu.VMEM((terms, rows, width), bf16) for rows in heights],
+            pltpu.VMEM((terms, max(heights), width), bf16),
+            *[pltpu.VMEM((ndev, CAP, rows, width), bf16) for rows in heights],
+            pltpu.VMEM((8, size), jnp.int32),
             pltpu.VMEM((orb_rows, points), f32),
             pltpu.VMEM((2 * orb_rows, points // 2), bf16),
             pltpu.VMEM((ncol, 2 * orb_rows, points // 2), bf16),
@@ -370,9 +381,9 @@
             dma((ncol,)),
             dma((ndev,)),
             dma((ndev,)),
-            dma((2, ndev)),
-            dma((2, ndev)),
-            dma((5,)),
+            dma((3, ndev)),
+            dma((3, ndev)),
+            dma((8,)),
         ],
         compiler_params=pltpu.CompilerParams(
             collective_id=0, has_side_effects=True, vmem_limit_bytes=EXCHANGE_BYTES
@@ -382,24 +393,20 @@
 
 
 def blocks_kernel(
-    lists_ref,
+    lists_smem,
     recv_ref,
     basis_ref,
     local_ref,
     out_ref,
-    lists_smem,
     inner_t,
     sums,
     joined_a,
     joined_b,
     formed,
     sems,
-    lists_sem,
 ):
     f32 = jnp.float32
     steps = local_ref.shape[0] // BLOCKS_STEP
-    lists_copy = pltpu.make_async_copy(lists_ref, lists_smem, lists_sem)
-    lists_copy.start()
     inner_t[...] = basis_ref[: recv_ref.shape[1], :].astype(f32).T.astype(jnp.bfloat16)
 
     def leave(step):
@@ -414,12 +421,10 @@
 
     def join(step, joined, i):
         head, follower, third = slots_of(step, i)
-        one = recv_ref[jnp.maximum(head, 0)].astype(f32)
-        two = recv_ref[jnp.maximum(follower, 0)].astype(f32)
+        one = recv_ref[jnp.maximum(head, 0)]
+        two = recv_ref[jnp.maximum(follower, 0)]
         nothing = jnp.zeros_like(one)
-        joined[i] = (
-            jnp.where(head < 0, nothing, one) + jnp.where(follower < 0, nothing, two)
-        ).astype(joined.dtype)
+        joined[i] = jnp.where(head < 0, nothing, one) + jnp.where(follower < 0, nothing, two)
         return third
 
     def multiply(step, joined, i):
@@ -463,7 +468,6 @@
         work(2 * pair + 1, joined_b, joined_a)
         return carried
 
-    lists_copy.wait()
     longest = jnp.int32(-1)
     for i in range(BLOCKS_STEP):
         longest = jnp.maximum(longest, join(0, joined_a, i))
@@ -484,21 +488,19 @@
     return pl.pallas_call(
         blocks_kernel,
         in_specs=[
-            pl.BlockSpec(memory_space=pl.ANY),
+            pl.BlockSpec(memory_space=pltpu.SMEM),
             vmem,
             vmem,
             vmem,
         ],
         out_specs=pl.BlockSpec(memory_space=pl.ANY),
         scratch_shapes=[
-            pltpu.SMEM(lists.shape, jnp.int32),
             pltpu.VMEM((width, inner), jnp.bfloat16),
             pltpu.VMEM((inner, width), jnp.float32),
             pltpu.VMEM((BLOCKS_STEP, inner, width), jnp.bfloat16),
             pltpu.VMEM((BLOCKS_STEP, inner, width), jnp.bfloat16),
             pltpu.VMEM((blocks, width, width), jnp.bfloat16),
             pltpu.SemaphoreType.DMA((blocks // BLOCKS_STEP,)),
-            pltpu.SemaphoreType.DMA,
         ],
         out_shape=jax.ShapeDtypeStruct((blocks, width, width), jnp.bfloat16),
         compiler_params=pltpu.CompilerParams(vmem_limit_bytes=BLOCKS_BYTES),

time: 113 us -> 109 us (0.965)
  Pallas kernels: 111 us -> 109 us
    pallas_call x1, Pallas kernels: 7.24 us -> 5.56 us  [make_blocks(): pl.pallas_call(blocks_kernel, in_specs=[pl.BlockSpec(memory_space=pltpu.S...]
where the time goes in v5:
time: 109 us
  Pallas kernels  109 us (100%)
    pallas_call x1, Pallas kernels, exchange(): pl.pallas_call(functools.partial(exchange_kernel, nrow, ncol), out_shape=...  103 us
    pallas_call x1, Pallas kernels, make_blocks(): pl.pallas_call(blocks_kernel, in_specs=[pl.BlockSpec(memory_space=pltpu.S...  5.56 us

profile of v5, /device:TPU:0, one launch (start us, length us, event | category | flops | bytes accessed | tf_op | source)
XLA Modules:
  0.0 109.1 jit_solution(13721513357799950157)
XLA Ops:
  0.0 0.0 copy-start
  0.0 103.5 %exchange.1 = (bf16[32,2,128,256]{3,2,1,0:T(8,128)(2,1)S(1)}, bf16[64,256,256]{2,1,0:T(8,128)(2,1)S(1)}, s32[8,128]{1,0:T(8,128)S(4)}) custom-call(bf16[192,128,256]{2,1,0:T(8,128)(2,1)} %ops_ref.1, bf16[8,512]{1,0:T(8,128)(2,1)} %orb_ref.1, f32[8,512]{1,0:T(8,128)} %pot_ref.1, s32[1,128]{1,0:T(1,128)} %bitcast.12, s32[1,192]{1,0:T(1,128)} %bitcast.11, ...), custom_call_target="tpu_custom_call" | custom-call | tf_op jit(solution)/shard_map/exchange/pallas_call | solution.py:356
  103.5 0.0 copy-done
  103.5 5.6 %make_blocks.1 = bf16[64,256,256]{2,1,0:T(8,128)(2,1)} custom-call(s32[8,128]{1,0:T(8,128)S(4)} %get-tuple-element.8.lists_smem, bf16[64,128,256]{2,1,0:T(8,128)(2,1)S(1)} %bitcast.8, bf16[512,256]{1,0:T(8,128)(2,1)S(1)} %copy-done, bf16[64,256,256]{2,1,0:T(8,128)(2,1)S(1)} %get-tuple-element.10.local_ref), custom_call_target="tpu_custom_call" | custom-call | tf_op jit(solution)/shard_map/make_blocks/pallas_call | solution.py:488
Async XLA Ops:
  0.0 103.5 %copy-start = (bf16[512,256]{1,0:T(8,128)(2,1)S(1)}, bf16[512,256]{1,0:T(8,128)(2,1)}, u32[]{:S(2)}) copy-start(bf16[512,256]{1,0:T(8,128)(2,1)} %basis_ref.3) | copy-start | bytes 786436

commit v6 on v5

--- a/solution.py
+++ b/solution.py
@@ -129,13 +129,11 @@
     )
 
     def peer(t):
-        low = lax.rem(t, ncol)
-        mask = 0
-        for b in range(ncol.bit_length() - 1):
-            mask = mask * 2 + lax.rem(lax.div(low, 2**b), 2)
+        left = ndev - t
+        high = lax.div(left, nrow)
         return (
-            masked(p, lax.rem(lax.div(t, ncol) + t, nrow), nrow),
-            masked(q, mask, ncol),
+            masked(p, lax.rem(left + high, nrow), nrow),
+            masked(q, lax.rem(high, ncol), ncol),
         )
 
     def each(count, action):

time: 109 us -> 111 us (1.018)
  Pallas kernels: 109 us -> 111 us
    pallas_call x1, Pallas kernels: 103 us -> 105 us  [exchange(): pl.pallas_call(functools.partial(exchange_kernel, nrow, ncol), out_shape=...]
where the time goes in v6:
time: 111 us
  Pallas kernels  111 us (100%)
    pallas_call x1, Pallas kernels, exchange(): pl.pallas_call(functools.partial(exchange_kernel, nrow, ncol), out_shape=...  105 us
    pallas_call x1, Pallas kernels, make_blocks(): pl.pallas_call(blocks_kernel, in_specs=[pl.BlockSpec(memory_space=pltpu.S...  5.83 us

profile of v6, /device:TPU:0, one launch (start us, length us, event | category | flops | bytes accessed | tf_op | source)
XLA Modules:
  0.0 110.6 jit_solution(16686387479012211589)
XLA Ops:
  0.0 0.0 copy-start
  0.0 104.7 %exchange.1 = (bf16[32,2,128,256]{3,2,1,0:T(8,128)(2,1)S(1)}, bf16[64,256,256]{2,1,0:T(8,128)(2,1)S(1)}, s32[8,128]{1,0:T(8,128)S(4)}) custom-call(bf16[192,128,256]{2,1,0:T(8,128)(2,1)} %ops_ref.1, bf16[8,512]{1,0:T(8,128)(2,1)} %orb_ref.1, f32[8,512]{1,0:T(8,128)} %pot_ref.1, s32[1,128]{1,0:T(1,128)} %bitcast.12, s32[1,192]{1,0:T(1,128)} %bitcast.11, ...), custom_call_target="tpu_custom_call" | custom-call | tf_op jit(solution)/shard_map/exchange/pallas_call | solution.py:354
  104.7 0.0 copy-done
  104.8 5.8 %make_blocks.1 = bf16[64,256,256]{2,1,0:T(8,128)(2,1)} custom-call(s32[8,128]{1,0:T(8,128)S(4)} %get-tuple-element.8.lists_smem, bf16[64,128,256]{2,1,0:T(8,128)(2,1)S(1)} %bitcast.8, bf16[512,256]{1,0:T(8,128)(2,1)S(1)} %copy-done, bf16[64,256,256]{2,1,0:T(8,128)(2,1)S(1)} %get-tuple-element.10.local_ref), custom_call_target="tpu_custom_call" | custom-call | tf_op jit(solution)/shard_map/make_blocks/pallas_call | solution.py:486
Async XLA Ops:
  0.0 104.7 %copy-start = (bf16[512,256]{1,0:T(8,128)(2,1)S(1)}, bf16[512,256]{1,0:T(8,128)(2,1)}, u32[]{:S(2)}) copy-start(bf16[512,256]{1,0:T(8,128)(2,1)} %basis_ref.3) | copy-start | bytes 786436
